TPU v7x, 32 devices: a whole 2x2x4 slice. The times are simulated.
32 devices in a mesh: batch: 8 (over z, y), seq: 4 (over x, core).
Axes of the slice: x: 2, y: 2, z: 4, core: 2. Of those that a mesh axis runs over, the one named last changes fastest.
Arguments:
- tokens: bfloat16 [8, 512, 1280], P('batch', 'seq'), may hold values from -26 to 26
- query_key_value_weight: bfloat16 [1280, 3840], P(('batch', 'seq')), may hold values from -0.15625 to 0.15625
- attention_output_weight: bfloat16 [1280, 1280], P(('batch', 'seq')), may hold values from -1 to 1
- up_projection_weight: bfloat16 [1280, 1280], P(('batch', 'seq')), may hold values from -0.15625 to 0.15625
- down_projection_weight: bfloat16 [1280, 1280], P(('batch', 'seq')), may hold values from -0.15625 to 0.15625
- gain_attn: bfloat16 [1280], P(('batch', 'seq')), may hold values from 0.25 to 1.75
- gain_ffn: bfloat16 [1280], P(('batch', 'seq')), may hold values from 0.25 to 1.75
- up_projection_bias: bfloat16 [1280], P(('batch', 'seq')), may hold values from -3 to 3
- down_projection_bias: bfloat16 [1280], P(('batch', 'seq')), may hold values from -2 to 2
- scale_param: bfloat16 [80], replicated, may hold values from -0.5 to 1.5
- cotangent: bfloat16 [8, 512, 1280], P('batch', 'seq'), may hold values from -6 to 6
Outputs:
- mixed: bfloat16 [8, 512, 1280], P('batch', 'seq')
- grad_tokens: float32 [8, 512, 1280], P('batch', 'seq')
- grad_qkv: float32 [1280, 3840], P(('batch', 'seq'))
- grad_out: float32 [1280, 1280], P(('batch', 'seq'))
- grad_up: float32 [1280, 1280], P(('batch', 'seq'))
- grad_down: float32 [1280, 1280], P(('batch', 'seq'))
- grad_gain_attn: float32 [1280], P(('batch', 'seq'))
- grad_gain_ffn: float32 [1280], P(('batch', 'seq'))
- grad_bias_up: float32 [1280], P(('batch', 'seq'))
- grad_bias_down: float32 [1280], P(('batch', 'seq'))
- grad_scale: float32 [80], replicated
All inputs are finite; a program needn't handle non-finite values.
Results may differ from a plain program's by a relative error of at most 0.025.
Values may be sent and summed in bfloat16 or wider, within the bound.
A program may use at most 192 MiB of HBM per device.

v0:
```python
import math

import jax
import jax.numpy as jnp
from jax import lax
from jax.sharding import PartitionSpec as P

H = 16
HD = 80


epsilon = 1e-06
soft_unit = 1.442695041
neg_large = -1e30


def norm_forward(values, gain):
    inverse = lax.rsqrt(jnp.mean(values * values, axis=1, keepdims=True) + epsilon)
    return (inverse, (values * inverse * gain.astype(jnp.float32)).astype(jnp.bfloat16))


def norm_back(grad_out, values, inverse, gain):
    normed = values * inverse
    scaled = grad_out * gain.astype(jnp.float32)
    grad_gain = jnp.sum(grad_out * normed, axis=0)
    grad_in = inverse * (scaled - normed * jnp.mean(scaled * normed, axis=1, keepdims=True))
    return (grad_in, grad_gain)


def body(
    tokens,
    query_key_value_weight,
    attention_output_weight,
    up_projection_weight,
    down_projection_weight,
    gain_attn,
    gain_ffn,
    up_projection_bias,
    down_projection_bias,
    scale_param,
    cotangent,
):
    seq_local, tok_seq, width = tokens.shape
    row_count = seq_local * tok_seq
    shards = (
        query_key_value_weight,
        attention_output_weight,
        up_projection_weight,
        down_projection_weight,
        gain_attn,
        gain_ffn,
        up_projection_bias,
        down_projection_bias,
    )
    fwd_weights = (
        lax.all_gather(shards[0], ("batch", "seq"), axis=0, tiled=True),
        lax.all_gather(shards[1], ("batch", "seq"), axis=0, tiled=True),
        lax.all_gather(shards[2], ("batch", "seq"), axis=0, tiled=True),
        lax.all_gather(shards[3], ("batch", "seq"), axis=0, tiled=True),
        lax.all_gather(shards[4], ("batch", "seq"), axis=0, tiled=True),
        lax.all_gather(shards[5], ("batch", "seq"), axis=0, tiled=True),
        lax.all_gather(shards[6], ("batch", "seq"), axis=0, tiled=True),
        lax.all_gather(shards[7], ("batch", "seq"), axis=0, tiled=True),
    )
    wqkv_full, wout_full, wup_full, wdown_full, gattn_full, gffn_full, bup_full, bdown_full = (
        fwd_weights
    )
    inputs = tokens.astype(jnp.float32).reshape(row_count, width)
    inv_attn, attention_normed_input = norm_forward(inputs, gattn_full)
    query_key_value = jnp.dot(attention_normed_input, wqkv_full, preferred_element_type=jnp.float32)
    q_raw = query_key_value[:, :width]
    scale_float = scale_param.astype(jnp.float32)
    factor = soft_unit / math.sqrt(HD) * jax.nn.softplus(scale_float)
    factor_row = jnp.tile(factor, H)
    queries = (q_raw * factor_row).astype(jnp.bfloat16)
    keys_own = (
        query_key_value[:, width : 2 * width]
        .astype(jnp.bfloat16)
        .reshape(seq_local, tok_seq, width)
    )
    values_own = (
        query_key_value[:, 2 * width :].astype(jnp.bfloat16).reshape(seq_local, tok_seq, width)
    )
    keys_all, values_all = (
        lax.all_gather(keys_own, "seq", axis=1, tiled=True),
        lax.all_gather(values_own, "seq", axis=1, tiled=True),
    )
    position = lax.axis_index("seq")
    block_total = lax.axis_size("seq")
    query_pos = position * tok_seq + jnp.arange(tok_seq, dtype=jnp.int32)
    key_offsets = jnp.arange(tok_seq, dtype=jnp.int32)
    queries_h = queries.reshape(seq_local, tok_seq, H, HD)

    def key_block(source, block):
        piece = lax.dynamic_slice_in_dim(source, block * tok_seq, tok_seq, 1)
        return piece.reshape(seq_local, tok_seq, H, HD)

    def block_scores(block):
        scores = jnp.einsum(
            "sqhd,skhd->shqk",
            queries_h,
            key_block(keys_all, block),
            preferred_element_type=jnp.float32,
        )
        allowed = (block * tok_seq + key_offsets)[None, :] <= query_pos[:, None]
        return jnp.where(allowed, scores, neg_large)

    def max_step(block, carry):
        top, total = carry
        scores = block_scores(block)
        new_top = jnp.maximum(top, jnp.max(scores, axis=3, keepdims=True))
        total = total * jnp.exp(top - new_top) + jnp.sum(
            jnp.exp(scores - new_top), axis=3, keepdims=True
        )
        return (new_top, total)

    start_top = jnp.full((seq_local, H, tok_seq, 1), neg_large, jnp.float32)
    top, total = lax.fori_loop(0, block_total, max_step, (start_top, jnp.zeros_like(start_top)))
    log_sum = top + jnp.log(total)

    def value_step(block, accum):
        probs = jnp.exp(block_scores(block) - log_sum).astype(jnp.bfloat16)
        return accum + jnp.einsum(
            "shqk,skhd->sqhd",
            probs,
            key_block(values_all, block),
            preferred_element_type=jnp.float32,
        )

    attention_output = lax.fori_loop(
        0, block_total, value_step, jnp.zeros((seq_local, tok_seq, H, HD), jnp.float32)
    )
    attention_output = attention_output.reshape(row_count, width)
    att_low = attention_output.astype(jnp.bfloat16)
    middle = inputs + jnp.dot(att_low, wout_full, preferred_element_type=jnp.float32)
    inv_ffn, feedforward_normed_input = norm_forward(middle, gffn_full)
    up_projected_value = jnp.dot(
        feedforward_normed_input, wup_full, preferred_element_type=jnp.float32
    ) + bup_full.astype(jnp.float32)
    act_low = jax.nn.silu(up_projected_value).astype(jnp.bfloat16)
    result = (
        middle
        + jnp.dot(act_low, wdown_full, preferred_element_type=jnp.float32)
        + bdown_full.astype(jnp.float32)
    )
    mixed = result.astype(jnp.bfloat16).reshape(seq_local, tok_seq, width)
    back_weights = (
        lax.all_gather(shards[0], ("batch", "seq"), axis=0, tiled=True),
        lax.all_gather(shards[1], ("batch", "seq"), axis=0, tiled=True),
        lax.all_gather(shards[2], ("batch", "seq"), axis=0, tiled=True),
        lax.all_gather(shards[3], ("batch", "seq"), axis=0, tiled=True),
        lax.all_gather(shards[4], ("batch", "seq"), axis=0, tiled=True),
        lax.all_gather(shards[5], ("batch", "seq"), axis=0, tiled=True),
        lax.all_gather(shards[6], ("batch", "seq"), axis=0, tiled=True),
        lax.all_gather(shards[7], ("batch", "seq"), axis=0, tiled=True),
    )
    wqkv_back, wout_back, wup_back, wdown_back, gattn_back, gffn_back, bup_back, bdown_back = (
        back_weights
    )
    grad_low = cotangent.reshape(row_count, width)
    grad_float = grad_low.astype(jnp.float32)
    grad_down = jnp.einsum("rf,rd->fd", act_low, grad_low, preferred_element_type=jnp.float32)
    grad_bias_down = jnp.sum(grad_float, axis=0)
    grad_act = jnp.einsum("rd,fd->rf", grad_low, wdown_back, preferred_element_type=jnp.float32)
    sigma = jax.nn.sigmoid(up_projected_value)
    grad_upv = (grad_act * sigma * (1.0 + up_projected_value * (1.0 - sigma))).astype(jnp.bfloat16)
    grad_up = jnp.einsum(
        "rd,rf->df", feedforward_normed_input, grad_upv, preferred_element_type=jnp.float32
    )
    grad_bias_up = jnp.sum(grad_upv.astype(jnp.float32), axis=0)
    grad_hn_ffn = jnp.einsum("rf,df->rd", grad_upv, wup_back, preferred_element_type=jnp.float32)
    grad_norm_ffn, grad_gain_ffn = norm_back(grad_hn_ffn, middle, inv_ffn, gffn_back)
    grad_middle = grad_float + grad_norm_ffn
    grad_attn = grad_middle.astype(jnp.bfloat16)
    grad_out = jnp.einsum("rd,re->de", att_low, grad_attn, preferred_element_type=jnp.float32)
    block_summed = (
        lax.psum_scatter(grad_out, ("batch", "seq"), scatter_dimension=0, tiled=True),
        lax.psum_scatter(grad_up, ("batch", "seq"), scatter_dimension=0, tiled=True),
        lax.psum_scatter(grad_down, ("batch", "seq"), scatter_dimension=0, tiled=True),
        lax.psum_scatter(grad_gain_ffn, ("batch", "seq"), scatter_dimension=0, tiled=True),
        lax.psum_scatter(grad_bias_up, ("batch", "seq"), scatter_dimension=0, tiled=True),
        lax.psum_scatter(grad_bias_down, ("batch", "seq"), scatter_dimension=0, tiled=True),
    )
    grad_att_low = jnp.einsum(
        "re,de->rd", grad_attn, wout_back, preferred_element_type=jnp.float32
    ).astype(jnp.bfloat16)
    grad_heads = grad_att_low.reshape(seq_local, tok_seq, H, HD)
    delta = jnp.sum(
        (grad_att_low.astype(jnp.float32) * attention_output).reshape(seq_local, tok_seq, H, HD),
        axis=3,
    )
    delta = jnp.transpose(delta, (0, 2, 1))[..., None]
    query_init = jnp.zeros((seq_local, tok_seq, H, HD), jnp.float32)

    def grad_step(block, carry):
        grad_query, term = carry
        scores = block_scores(block)
        probs = jnp.exp(scores - log_sum)
        keys_blk = key_block(keys_all, block)
        values_blk = key_block(values_all, block)
        grad_probs = jnp.einsum(
            "sqhd,skhd->shqk", grad_heads, values_blk, preferred_element_type=jnp.float32
        )
        grad_scores = (probs * (grad_probs - delta)).astype(jnp.bfloat16)
        grad_values = jnp.einsum(
            "shqk,sqhd->skhd",
            probs.astype(jnp.bfloat16),
            grad_heads,
            preferred_element_type=jnp.float32,
        )
        grad_keys = jnp.einsum(
            "shqk,sqhd->skhd", grad_scores, queries_h, preferred_element_type=jnp.float32
        )
        grad_query = grad_query + jnp.einsum(
            "shqk,skhd->sqhd", grad_scores, keys_blk, preferred_element_type=jnp.float32
        )
        piece = jnp.concatenate(
            [
                grad_keys.reshape(seq_local, tok_seq, width),
                grad_values.reshape(seq_local, tok_seq, width),
            ],
            axis=2,
        )
        term = lax.dynamic_update_slice_in_dim(term, piece, block * tok_seq, 1)
        return (grad_query, term)

    term_init = jnp.zeros((seq_local, tok_seq * block_total, 2 * width), jnp.float32)
    grad_query, term = lax.fori_loop(0, block_total, grad_step, (query_init, term_init))
    kv_grads = lax.psum_scatter(
        term.astype(jnp.bfloat16), "seq", scatter_dimension=1, tiled=True
    ).astype(jnp.float32)
    grad_scaled = grad_query.reshape(row_count, width)
    scale_local = jnp.sum((grad_scaled * q_raw).reshape(row_count, H, HD), axis=(0, 1))
    scale_total = lax.psum(scale_local, ("batch", "seq"))
    grad_scale = scale_total * (soft_unit / math.sqrt(HD)) * jax.nn.sigmoid(scale_float)
    grad_qkv_low = jnp.concatenate(
        [grad_scaled * factor_row, kv_grads.reshape(row_count, 2 * width)], axis=1
    ).astype(jnp.bfloat16)
    grad_qkv = jnp.einsum(
        "rd,re->de", attention_normed_input, grad_qkv_low, preferred_element_type=jnp.float32
    )
    grad_hn_attn = jnp.einsum(
        "re,de->rd", grad_qkv_low, wqkv_back, preferred_element_type=jnp.float32
    )
    grad_norm_attn, grad_gain_attn = norm_back(grad_hn_attn, inputs, inv_attn, gattn_back)
    grad_tokens = (grad_middle + grad_norm_attn).reshape(seq_local, tok_seq, width)
    qkv_summed = (
        lax.psum_scatter(grad_qkv, ("batch", "seq"), scatter_dimension=0, tiled=True),
        lax.psum_scatter(grad_gain_attn, ("batch", "seq"), scatter_dimension=0, tiled=True),
    )
    return (
        mixed,
        grad_tokens,
        qkv_summed[0],
        block_summed[0],
        block_summed[1],
        block_summed[2],
        qkv_summed[1],
        block_summed[3],
        block_summed[4],
        block_summed[5],
        grad_scale,
    )


def solution(mesh):
    return jax.shard_map(
        body,
        mesh=mesh,
        in_specs=(
            P("batch", "seq", None),
            P(("batch", "seq"), None),
            P(("batch", "seq"), None),
            P(("batch", "seq"), None),
            P(("batch", "seq"), None),
            P(("batch", "seq")),
            P(("batch", "seq")),
            P(("batch", "seq")),
            P(("batch", "seq")),
            P(),
            P("batch", "seq", None),
        ),
        out_specs=(
            P("batch", "seq", None),
            P("batch", "seq", None),
            P(("batch", "seq"), None),
            P(("batch", "seq"), None),
            P(("batch", "seq"), None),
            P(("batch", "seq"), None),
            P(("batch", "seq")),
            P(("batch", "seq")),
            P(("batch", "seq")),
            P(("batch", "seq")),
            P(),
        ),
        check_vma=False,
    )
```

profile of v0, /device:TPU:0, one launch (start us, length us, event | category | flops | bytes accessed | tf_op | source)
XLA Modules:
  0.0 1067.7 jit_solution(17451013476676559857)
XLA Ops:
  11.4 43.4 %all-reduce.9 = (bf16[1280]{0:T(1024)(128)(2,1)S(1)}, bf16[1280]{0:T(1024)(128)(2,1)}, bf16[1280]{0:T(1024)(128)(2,1)S(1)}, bf16[1280]{0:T(1024)(128)(2,1)S(1)}) all-reduce(bf16[1280]{0:T(1024)(128)(2,1)S(1)} %dynamic-update-slice, bf16[1280]{0:T(1024)(128)(2,1)S(1)} %dynamic-update-slice.3, ...), channel_id=1, replica_groups=mesh['batch'=8,'seq'=4] {'batch','seq'}, use_global_device_ids=true, to_apply=%add | all-reduce | flops 5120 | bytes 20480
  56.0 41.9 %all-gather.9.cloned.1.call-done = bf16[1280,3840]{1,0:T(8,128)(2,1)} async-done(((bf16[40,3840]{1,0:T(8,128)(2,1)}), bf16[1280,3840]{1,0:T(8,128)(2,1)}) %all-gather.9.cloned.1.call-update) | async-done | bytes 9830416 | tf_op jit(solution)/shard_map/all_gather | solution.py:56
  97.9 6.8 fusion.75
  109.8 12.7 %all-gather.19.cloned.1.call-done = bf16[512,1280]{1,0:T(8,128)(2,1)} async-done(((bf16[128,1280]{1,0:T(8,128)(2,1)}), bf16[512,1280]{1,0:T(8,128)(2,1)}) %all-gather.19.cloned.1.call-update) | async-done | bytes 1310736 | tf_op jit(solution)/shard_map/all_gather | solution.py:85
  124.9 6.8 while.46
  131.7 11.1 %all-gather.17.cloned.1.call-done = bf16[512,1280]{1,0:T(8,128)(2,1)} async-done(((bf16[128,1280]{1,0:T(8,128)(2,1)}), bf16[512,1280]{1,0:T(8,128)(2,1)}) %all-gather.17.cloned.1.call-update) | async-done | bytes 1310736 | tf_op jit(solution)/shard_map/all_gather | solution.py:86
  145.9 10.6 while.47
  157.6 47.3 %all-gather.11.cloned.1.call-done = bf16[1280,1280]{1,0:T(8,128)(2,1)} async-done(((bf16[40,1280]{1,0:T(8,128)(2,1)}), bf16[1280,1280]{1,0:T(8,128)(2,1)}) %all-gather.11.cloned.1.call-update) | async-done | bytes 3276816 | tf_op jit(solution)/shard_map/all_gather | solution.py:57
  207.5 58.2 %all-gather.13.cloned.1.call-done = bf16[1280,1280]{1,0:T(8,128)(2,1)} async-done(((bf16[40,1280]{1,0:T(8,128)(2,1)}), bf16[1280,1280]{1,0:T(8,128)(2,1)}) %all-gather.13.cloned.1.call-update) | async-done | bytes 3276816 | tf_op jit(solution)/shard_map/all_gather | solution.py:58
  269.1 57.4 %all-gather.15.cloned.1.call-done = bf16[1280,1280]{1,0:T(8,128)(2,1)} async-done(((bf16[40,1280]{1,0:T(8,128)(2,1)}), bf16[1280,1280]{1,0:T(8,128)(2,1)}) %all-gather.15.cloned.1.call-update) | async-done | bytes 3276816 | tf_op jit(solution)/shard_map/all_gather | solution.py:59
  326.6 4.1 convert_reduce_fusion.1
  338.7 19.8 %while.48 = (s32[]{:T(128)}, f32[1,128,16,80]{1,3,2,0:T(8,128)S(1)}, bf16[1,512,2560]{1,2,0:T(8,128)(2,1)}, bf16[1,512,1280]{1,2,0:T(8,128)(2,1)}, bf16[1,128,16...) while((s32[]{:T(128)}, ...), condition=%wide.region_11.12_spmd.clone, body=%wide.region_10.11_spmd.clone.sunk | while | flops 212943104 | bytes 11651285 | solution.py:228
  358.5 11.4 %copy.87 = bf16[1,512,2560]{2,0,1:T(2,128)(2,1)} copy(bf16[1,512,2560]{1,2,0:T(8,128)(2,1)} %get-tuple-element.464) | data formatting | bytes 5242880
  369.9 4.6 copy.91
  380.5 3.8 fusion.72
  385.5 3.8 fusion.58
  393.0 15.3 %reduce-scatter.16.cloned.1.call-done = bf16[128,2560]{1,0:T(8,128)(2,1)} async-done(((bf16[512,2560]{1,0:T(8,128)(2,1)}), bf16[128,2560]{1,0:T(8,128)(2,1)}) %reduce-scatter.16.cloned.1.call-update) | async-done | bytes 655376
  413.6 8.3 fusion.56
  426.0 7.3 fusion.54
  433.3 41.6 %all-reduce.8 = (f32[1280]{0:T(1024)S(1)}, f32[1280]{0:T(1024)S(1)}, f32[1280]{0:T(1024)S(1)}, f32[1280]{0:T(1024)S(1)}, f32[80]{0:T(128)S(1)}) all-reduce(f32[1280]{0:T(1024)S(1)} %get-tuple-element.652, f32[1280]{0:T(1024)S(1)} %copy-done.21, f32[1280]{0:T(1024)S(1)} %copy-done.27, ...), channel_id=9, replica_groups=mesh['batch'=8,'seq'=4] {'batch','seq'}, use_global_device_ids=true, to_apply=%region_19.20.clone | all-reduce | flops 5200 | bytes 41600
  478.9 78.0 %reduce-scatter.10.cloned.1.call-done = f32[40,1280]{1,0:T(8,128)} async-done(((f32[1280,1280]{1,0:T(8,128)}), f32[40,1280]{1,0:T(8,128)}) %reduce-scatter.10.cloned.1.call-update) | async-done | bytes 204816 | tf_op jit(solution)/shard_map/reduce_scatter | solution.py:177
  556.9 144.4 %reduce-scatter.12.cloned.1.call-done = f32[40,1280]{1,0:T(8,128)} async-done(((f32[1280,1280]{1,0:T(8,128)}), f32[40,1280]{1,0:T(8,128)}) %reduce-scatter.12.cloned.1.call-update) | async-done | bytes 204816 | tf_op jit(solution)/shard_map/reduce_scatter | solution.py:178
  701.2 144.2 %reduce-scatter.14.cloned.1.call-done = f32[40,1280]{1,0:T(8,128)} async-done(((f32[1280,1280]{1,0:T(8,128)}), f32[40,1280]{1,0:T(8,128)}) %reduce-scatter.14.cloned.1.call-update) | async-done | bytes 204816 | tf_op jit(solution)/shard_map/reduce_scatter | solution.py:179
  845.4 215.7 %reduce-scatter.8.cloned.1.call-done = f32[40,3840]{1,0:T(8,128)} async-done(((f32[1280,3840]{1,0:T(8,128)}), f32[40,3840]{1,0:T(8,128)}) %reduce-scatter.8.cloned.1.call-update) | async-done | bytes 614416 | tf_op jit(solution)/shard_map/reduce_scatter | solution.py:248
  (223 shorter events, 91.8 us)
Async XLA Ops:
  7.2 90.7 %all-gather.9.cloned.1.call-start = ((), (), s32[]{:S(2)}) async-start(), calls=%async_computation.5 | async-start | bytes 10137600 | tf_op jit(solution)/shard_map/all_gather | solution.py:56
  7.9 114.5 %all-gather.19.cloned.1.call-start = ((), (), s32[]{:S(2)}) async-start(), calls=%async_computation.14 | async-start | bytes 1638400 | tf_op jit(solution)/shard_map/all_gather | solution.py:85
  56.0 48.7 %copy-start.23 = (f32[128]{0:T(128)}, f32[128]{0:T(128)S(1)}, u32[]{:S(2)}) copy-start(f32[128]{0:T(128)S(1)} %add_rsqrt_fusion.1) | copy-start | bytes 1540
  56.0 52.3 %copy-start.29 = (bf16[80]{0:T(256)(128)(2,1)S(1)}, bf16[80]{0:T(256)(128)(2,1)}, u32[]{:S(2)}) copy-start(bf16[80]{0:T(256)(128)(2,1)} %param.26) | copy-start | bytes 484
  105.6 37.3 %all-gather.17.cloned.1.call-start = ((), (), s32[]{:S(2)}) async-start(), calls=%async_computation.13 | async-start | bytes 1638400 | tf_op jit(solution)/shard_map/all_gather | solution.py:86
  106.3 98.5 %all-gather.11.cloned.1.call-start = ((), (), s32[]{:S(2)}) async-start(), calls=%async_computation.6 | async-start | bytes 3379200 | tf_op jit(solution)/shard_map/all_gather | solution.py:57
  106.9 158.8 %all-gather.13.cloned.1.call-start = ((), (), s32[]{:S(2)}) async-start(), calls=%async_computation.7 | async-start | bytes 3379200 | tf_op jit(solution)/shard_map/all_gather | solution.py:58
  107.5 219.1 %all-gather.15.cloned.1.call-start = ((), (), s32[]{:S(2)}) async-start(), calls=%async_computation.8 | async-start | bytes 3379200 | tf_op jit(solution)/shard_map/all_gather | solution.py:59
  108.0 300.2 %reduce-scatter.16.cloned.1.call-start = ((), (), s32[]{:S(2)}) async-start(), calls=%async_computation.15 | async-start | bytes 3276800
  108.4 16.5 %copy-start.19 = (f32[1280]{0:T(1024)}, f32[1280]{0:T(1024)S(1)}, u32[]{:S(2)}) copy-start(f32[1280]{0:T(1024)S(1)} %mul.195) | copy-start | bytes 15364
  108.4 224.1 %copy-start.17 = (f32[1280]{0:T(1024)}, f32[1280]{0:T(1024)S(1)}, u32[]{:S(2)}) copy-start(f32[1280]{0:T(1024)S(1)} %convert_element_type.90) | copy-start | bytes 15364
  145.9 59.0 %copy-start.4 = (bf16[1,128,1280]{2,1,0:T(8,128)(2,1)S(1)}, bf16[1,128,1280]{2,1,0:T(8,128)(2,1)}, u32[]{:S(2)}) copy-start(bf16[1,128,1280]{2,1,0:T(8,128)(2,1)} %param.17) | copy-start | bytes 983044
  156.4 112.7 %copy-start.7 = (f32[1,128,16,80]{1,3,2,0:T(8,128)}, f32[1,128,16,80]{1,3,2,0:T(8,128)S(1)}, u32[]{:S(2)}) copy-start(f32[1,128,16,80]{1,3,2,0:T(8,128)S(1)} %get-tuple-element.462) | copy-start | bytes 1966084
  207.5 125.0 %copy-start = (f32[128,1280]{1,0:T(8,128)}, f32[128,1280]{1,0:T(8,128)S(1)}, u32[]{:S(2)}) copy-start(f32[128,1280]{1,0:T(8,128)S(1)} %get-tuple-element.730) | copy-start | bytes 1966084
  207.5 119.1 %copy-start.11 = (bf16[1,128,1280]{2,1,0:T(8,128)(2,1)S(1)}, bf16[1,128,1280]{2,1,0:T(8,128)(2,1)}, u32[]{:S(2)}) copy-start(bf16[1,128,1280]{2,1,0:T(8,128)(2,1)} %param.27) | copy-start | bytes 983044
  207.5 125.0 %copy-start.25 = (f32[128]{0:T(128)}, f32[128]{0:T(128)S(1)}, u32[]{:S(2)}) copy-start(f32[128]{0:T(128)S(1)} %add_rsqrt_fusion) | copy-start | bytes 1540
  374.5 182.4 %reduce-scatter.10.cloned.1.call-start = ((), (), s32[]{:S(2)}) async-start(), calls=%async_computation.10 | async-start | bytes 6758400 | tf_op jit(solution)/shard_map/reduce_scatter | solution.py:177
  379.3 321.9 %reduce-scatter.12.cloned.1.call-start = ((), (), s32[]{:S(2)}) async-start(), calls=%async_computation.11 | async-start | bytes 6758400 | tf_op jit(solution)/shard_map/reduce_scatter | solution.py:178
  384.3 461.1 %reduce-scatter.14.cloned.1.call-start = ((), (), s32[]{:S(2)}) async-start(), calls=%async_computation.12 | async-start | bytes 6758400 | tf_op jit(solution)/shard_map/reduce_scatter | solution.py:179
  389.3 671.9 %reduce-scatter.8.cloned.1.call-start = ((), (), s32[]{:S(2)}) async-start(), calls=%async_computation.9 | async-start | bytes 20275200 | tf_op jit(solution)/shard_map/reduce_scatter | solution.py:248
  390.4 23.2 %copy-start.24 = (f32[128]{0:T(128)S(1)}, f32[128]{0:T(128)}, u32[]{:S(2)}) copy-start(f32[128]{0:T(128)} %copy-done.23) | copy-start | bytes 1540
  393.0 20.7 %copy-start.14 = (bf16[128,1280]{0,1:T(8,128)(2,1)S(1)}, bf16[128,1280]{0,1:T(8,128)(2,1)}, u32[]{:S(2)}) copy-start(bf16[128,1280]{0,1:T(8,128)(2,1)} %copy.81) | copy-start | bytes 983044
  426.0 7.3 copy-start.27
  426.0 51.2 %copy-start.30 = (bf16[80]{0:T(256)(128)(2,1)S(1)}, bf16[80]{0:T(256)(128)(2,1)}, u32[]{:S(2)}) copy-start(bf16[80]{0:T(256)(128)(2,1)} %param.26) | copy-start | bytes 484
  (18 other events, 45.9 us)
Sparse Core Ops, SparseCore 0:
  10.9 86.9 all-gather.8
  105.7 16.7 all-gather.18
  124.6 18.1 all-gather.16
  145.5 59.2 all-gather.10
  207.5 58.1 all-gather.12
  268.4 58.1 all-gather.14
  374.6 33.5 reduce-scatter.15
  411.2 145.6 reduce-scatter.9
  559.9 141.3 reduce-scatter.11
  704.1 141.3 reduce-scatter.13
  853.6 207.5 reduce-scatter.7
where the time goes:
time: 1070 us
  waiting for transfers between devices  829 us (77%)
  blocking collectives  85 us (8%)
  matrix products  68.9 us (6%)
  local copies, waits for them, and re-layouts  56.2 us (5%)
  between operations  14.2 us (1%)
  other arithmetic  12.7 us (1%)
    reduce_scatter x1, waiting for transfers between devices, body(): lax.psum_scatter(grad_qkv, ('batch', 'seq'), scatter_dimension=0, tiled=T...  216 us
    reduce_scatter x1, waiting for transfers between devices, body(): lax.psum_scatter(grad_up, ('batch', 'seq'), scatter_dimension=0, tiled=True)  144 us
    reduce_scatter x1, waiting for transfers between devices, body(): lax.psum_scatter(grad_down, ('batch', 'seq'), scatter_dimension=0, tiled=...  144 us
    unnamed x2, blocking collectives  85 us
    reduce_scatter x1, waiting for transfers between devices, body(): lax.psum_scatter(grad_out, ('batch', 'seq'), scatter_dimension=0, tiled=T...  78 us
    all_gather x1, waiting for transfers between devices, body(): lax.all_gather(shards[2], ('batch', 'seq'), axis=0, tiled=True)  58.2 us
    all_gather x1, waiting for transfers between devices, body(): lax.all_gather(shards[3], ('batch', 'seq'), axis=0, tiled=True)  57.4 us
    all_gather x1, waiting for transfers between devices, body(): lax.all_gather(shards[1], ('batch', 'seq'), axis=0, tiled=True)  47.3 us
  transfers between devices with their start and end apart: 11, of which 11 were waited for; matrix products, arithmetic and copies ran while one was open for 7% of the time, Pallas kernels for 0%

commit v1 on v0

--- a/solution.py
+++ b/solution.py
@@ -1,8 +1,12 @@
+import functools
 import math
+import types
 
 import jax
 import jax.numpy as jnp
 from jax import lax
+from jax.experimental import pallas as pl
+from jax.experimental.pallas import tpu as pltpu
 from jax.sharding import PartitionSpec as P
 
 H = 16
@@ -27,7 +31,7 @@
     return (grad_in, grad_gain)
 
 
-def body(
+def generic_layer(
     tokens,
     query_key_value_weight,
     attention_output_weight,
@@ -263,9 +267,772 @@
     )
 
 
+MESH = pl.DeviceIdType.MESH
+F32 = jnp.float32
+BF16 = jnp.bfloat16
+
+
+def fits_fused(nb, ns, tokens, wqkv, wup):
+    rows, width = wup.shape[0], wup.shape[1]
+    return (
+        ns == 4
+        and nb % 2 == 0
+        and tokens.shape == (1, 128, H * HD)
+        and width == H * HD
+        and 2 * rows == HD
+        and nb * ns * rows == width
+        and wqkv.shape == (rows, 3 * width)
+    )
+
+
+def nt(a, b):
+    return lax.dot_general(a, b, (((1,), (1,)), ((), ())), preferred_element_type=F32)
+
+
+def nn(a, b):
+    return lax.dot_general(a, b, (((1,), (0,)), ((), ())), preferred_element_type=F32)
+
+
+def tn(a, b):
+    return lax.dot_general(a, b, (((0,), (0,)), ((), ())), preferred_element_type=F32)
+
+
+def layer_kernel(nz, scratch_names, tok, cot, w1p, w2p, smalls, scl, *refs):
+    mixed_o, gtok_o, o1, o2, sg_o = refs[:5]
+    r = types.SimpleNamespace(**dict(zip(scratch_names, refs[5:])))
+    D = tok.shape[1]
+    T = tok.shape[0]
+    L = 4 * T
+    HP = 2 * T
+    NH = 4
+    HW = NH * HD
+    CB = HD
+    RW = HD // 2
+    LO = 256
+    b = lax.axis_index("batch")
+    s = lax.axis_index("seq")
+    z, y = b // 2, b % 2
+    x, c = s // 2, s % 2
+    sib = (b, 2 * x + (1 - c))
+    xp = (b, 2 * (1 - x) + c)
+    yp = (2 * z + (1 - y), s)
+    zup = (lax.rem(2 * (z + 1), 2 * nz) + y, s)
+    zdn = (lax.rem(2 * (z + nz - 1), 2 * nz) + y, s)
+    drains = []
+
+    def when(cond, fn):
+        if cond is None:
+            fn()
+        else:
+            pl.when(cond)(fn)
+
+    def both(p, q):
+        if p is None:
+            return q
+        if q is None:
+            return p
+        return jnp.logical_and(p, q)
+
+    def copy(src, dst, ssem, rsem, dev):
+        return pltpu.make_async_remote_copy(
+            src_ref=src, dst_ref=dst, send_sem=ssem, recv_sem=rsem, device_id=dev, device_id_type=MESH
+        )
+
+    def send(make, cond=None):
+        when(cond, lambda: make().start())
+        drains.append((make, cond))
+
+    def arrive(make, cond=None):
+        when(cond, lambda: make().wait_recv())
+
+    bar = pltpu.get_barrier_semaphore()
+    peers = [sib, xp, yp]
+    for k in range(1, nz):
+        peers.append((2 * lax.rem(z + k, nz) + y, s))
+    for dev in peers:
+        pl.semaphore_signal(bar, inc=1, device_id=dev, device_id_type=MESH)
+    pl.semaphore_wait(bar, len(peers))
+
+    m_sib1 = lambda: copy(w1p.at[1 - c], r.SIB1, r.s_one.at[0], r.r_one.at[0], sib)
+    m_ssib = lambda: copy(smalls, r.S.at[b, s], r.s_one.at[1], r.r_one.at[1], sib)
+    m_sib2 = lambda: copy(w2p, r.SIB2, r.s_one.at[2], r.r_one.at[2], sib)
+    send(m_sib1)
+    send(m_ssib)
+    send(m_sib2)
+    r.S[b, s] = smalls[...]
+    r.X[s] = tok[...]
+    r.DY[s] = cot[...]
+
+    def chip_rows(own, other):
+        own, other = own[:RW].astype(F32), other[:RW].astype(F32)
+        lo = jnp.where(c == 0, own, other)
+        hi = jnp.where(c == 0, other, own)
+        return jnp.concatenate([lo, hi], axis=0).astype(BF16)
+
+    arrive(m_sib1)
+    r.CB1[...] = chip_rows(w1p[c, 1 - x], r.SIB1[1 - x])
+    m_x1 = lambda: copy(r.CB1, r.W1.at[b, x], r.s_one.at[3], r.r_one.at[3], xp)
+    send(m_x1)
+    r.W1[b, x] = chip_rows(w1p[c, x], r.SIB1[x])
+    m_ssib_r = lambda: copy(smalls, r.S.at[b, 2 * x + (1 - c)], r.s_one.at[1], r.r_one.at[1], sib)
+    arrive(m_ssib_r)
+    m_xs = lambda: copy(
+        r.S.at[b, pl.ds(2 * x, 2)], r.S.at[b, pl.ds(2 * x, 2)], r.s_one.at[4], r.r_one.at[4], xp
+    )
+    send(m_xs)
+    m_xt = lambda: copy(tok, r.X.at[s], r.s_one.at[5], r.r_one.at[5], xp)
+    m_st = lambda: copy(tok, r.X.at[s], r.s_one.at[6], r.r_one.at[6], sib)
+    m_xc = lambda: copy(cot, r.DY.at[s], r.s_one.at[7], r.r_one.at[7], xp)
+    m_sc = lambda: copy(cot, r.DY.at[s], r.s_one.at[8], r.r_one.at[8], sib)
+    send(m_xt)
+    send(m_st)
+    send(m_xc)
+    send(m_sc)
+    arrive(m_sib2)
+
+    def fill_w2():
+        r.W2[z] = chip_rows(w2p[...], r.SIB2[...])
+
+    mine = c == y
+    when(mine, fill_w2)
+
+    def gather_item(idx, block, zcond):
+        up = lambda zz: copy(block(zz, y), block(zz, y), r.s_up.at[idx, zz], r.r_up.at[idx, zz], zup)
+        dn = lambda zz: copy(block(zz, y), block(zz, y), r.s_dn.at[idx, zz], r.r_dn.at[idx, zz], zdn)
+        yy = lambda zz: copy(block(zz, y), block(zz, y), r.s_y.at[idx, zz], r.r_y.at[idx, zz], yp)
+
+        def start():
+            send(lambda: up(z), both(zcond, z < nz - 1))
+            send(lambda: dn(z), both(zcond, z > 0))
+            send(lambda: yy(z), zcond)
+
+        def step(d):
+            lo, hi = z - d, z + d
+            below, above = both(zcond, lo >= 0), both(zcond, hi < nz)
+            arrive(lambda: up(lo), below)
+            send(lambda: up(lo), both(below, z < nz - 1))
+            arrive(lambda: dn(hi), above)
+            send(lambda: dn(hi), both(above, z > 0))
+            send(lambda: yy(lo), below)
+            send(lambda: yy(hi), above)
+
+        def finish():
+            for k in range(nz):
+                when(
+                    None if zcond is None else jnp.logical_not(zcond),
+                    lambda k=k: copy(
+                        block(k, 1 - y), block(k, 1 - y), r.s_y.at[idx, k], r.r_y.at[idx, k], yp
+                    ).wait_recv(),
+                )
+
+        return start, step, finish
+
+    g_s = gather_item(0, lambda zz, q: r.S.at[2 * zz + q], None)
+    g_qkv = gather_item(1, lambda zz, q: r.W1.at[2 * zz + q, :, :, pl.ds(LO, D - LO)], None)
+    g_out = gather_item(2, lambda zz, q: r.W2.at[zz, :, pl.ds(0, D)], mine)
+    g_up = gather_item(3, lambda zz, q: r.W1.at[2 * zz + q, :, :, pl.ds(0, LO)], None)
+    g_dn = gather_item(4, lambda zz, q: r.W2.at[zz, :, pl.ds(D, D)], mine)
+
+    m_x1_r = lambda: copy(r.CB1, r.W1.at[b, 1 - x], r.s_one.at[3], r.r_one.at[3], xp)
+    m_xs_r = lambda: copy(
+        r.S.at[b, pl.ds(2 - 2 * x, 2)],
+        r.S.at[b, pl.ds(2 - 2 * x, 2)],
+        r.s_one.at[4],
+        r.r_one.at[4],
+        xp,
+    )
+    arrive(m_xs_r)
+    arrive(m_x1_r)
+    g_s[0]()
+    g_qkv[0]()
+    sx = 2 * (1 - x) + c
+    so = 2 * (1 - x) + (1 - c)
+    ss = 2 * x + (1 - c)
+    fwd = lambda name, k, src_i: copy(
+        name.at[src_i], name.at[src_i], r.s_one.at[k], r.r_one.at[k], sib
+    )
+    arrive(lambda: copy(tok, r.X.at[sx], r.s_one.at[5], r.r_one.at[5], xp))
+    send(lambda: fwd(r.X, 9, sx))
+    g_s[1](1)
+    g_qkv[1](1)
+    arrive(lambda: copy(cot, r.DY.at[sx], r.s_one.at[7], r.r_one.at[7], xp))
+    send(lambda: fwd(r.DY, 10, sx))
+    arrive(lambda: copy(tok, r.X.at[ss], r.s_one.at[6], r.r_one.at[6], sib))
+    arrive(lambda: fwd(r.X, 9, so))
+    arrive(lambda: copy(cot, r.DY.at[ss], r.s_one.at[8], r.r_one.at[8], sib))
+    arrive(lambda: fwd(r.DY, 10, so))
+    for d in range(2, nz):
+        g_s[1](d)
+        g_qkv[1](d)
+    g_out[0]()
+    g_up[0]()
+    g_dn[0]()
+    g_s[2]()
+
+    jf = lax.broadcasted_iota(jnp.int32, (1, D), 1).astype(F32)
+    jk = jnp.floor((jf + 0.5) / RW)
+    jl = jf - RW * jk
+    pick = (lax.broadcasted_iota(jnp.int32, (128, D), 0).astype(F32) == jl).astype(BF16)
+    sm_rows = 2 * nz * 4
+    spread = nn(r.S[...].reshape(sm_rows * 8, 128).astype(BF16), pick)
+    spread = spread.reshape(sm_rows, 8, D)
+    owner = lax.broadcasted_iota(jnp.int32, (sm_rows, 8, D), 0).astype(F32)
+    r.ROWS[...] = jnp.sum(jnp.where(owner == jk[None], spread, 0.0), axis=0)
+    uf = jf[:, :HW]
+    uj = jnp.floor((uf + 0.5) / HD)
+    uh = jnp.floor((uf - HD * uj + 0.5) / RW)
+    base = (2 * c + x).astype(F32)
+    uk = 2.0 * (4.0 * uj + base) + uh
+    r.BUP[...] = jnp.sum(
+        jnp.where(owner[:, :, :HW] == uk[None], spread[:, :, :HW], 0.0), axis=0
+    )
+    gain_attn = r.ROWS[0:1]
+    gain_ffn = r.ROWS[1:2]
+    bias_down = r.ROWS[3:4]
+    bias_up = r.BUP[2:3]
+    scale = scl[0:1, :]
+    factor = soft_unit / math.sqrt(HD) * (
+        jnp.maximum(scale, 0.0) + jnp.log(1.0 + jnp.exp(-jnp.abs(scale)))
+    )
+
+    for k in range(4):
+        xv = r.X[k].astype(F32)
+        inv = lax.rsqrt(jnp.mean(xv * xv, axis=1, keepdims=True) + epsilon)
+        hn = xv * inv * gain_attn
+        r.HN1[pl.ds(k * T, T)] = hn.astype(BF16)
+        r.HN1T[:, :, pl.ds(k * T, T)] = hn.T.astype(BF16).reshape(2 * nz, 2 * CB, T)
+    g_out[1](1)
+    g_qkv[2]()
+    g_up[1](1)
+
+    W1 = r.W1
+    W2 = r.W2
+    for h in range(2):
+        wq = W1[:, :, :, pl.ds(LO + 512 * h, 512)].reshape(D, 512)
+        r.QKV[:, pl.ds(512 * h, 512)] = nn(r.HN1[...], wq)
+    g_out[1](2)
+    g_up[1](2)
+    g_dn[1](1)
+    off = HW - LO
+    for j in range(NH):
+        q = r.QKV[:, off + HD * j : off + HD * (j + 1)]
+        k = r.QKV[:, off + HW + HD * j : off + HW + HD * (j + 1)]
+        v = r.QKV[:, off + 2 * HW + HD * j : off + 2 * HW + HD * (j + 1)]
+        r.QRAW[j] = q
+        r.QH[j] = (q * factor[:, :HD]).astype(BF16)
+        r.KH[j] = k.astype(BF16)
+        r.VH[j] = v.astype(BF16)
+        r.KT[j] = k.T.astype(BF16)
+        r.VT[j] = v.T.astype(BF16)
+    for d in range(3, nz):
+        g_out[1](d)
+        g_up[1](d)
+    if nz > 2:
+        g_dn[1](2)
+
+    tri_k = lax.broadcasted_iota(jnp.int32, (HP, HP), 0)
+    tri_q = lax.broadcasted_iota(jnp.int32, (HP, HP), 1)
+    seen = tri_k <= tri_q
+
+    def rows_of(p):
+        return pl.ds(p * HP, HP)
+
+    def attend(p, j):
+        q = r.QH[j, rows_of(p)]
+        diag = jnp.where(seen, nt(r.KH[j, rows_of(p)], q), neg_large)
+        top = jnp.max(diag, axis=0, keepdims=True)
+        if p:
+            full = nt(r.KH[j, pl.ds(0, HP)], q)
+            top = jnp.maximum(top, jnp.max(full, axis=0, keepdims=True))
+            full = jnp.exp(full - top)
+        diag = jnp.exp(diag - top)
+        total = jnp.sum(diag, axis=0, keepdims=True)
+        if p:
+            total = total + jnp.sum(full, axis=0, keepdims=True)
+        inv = 1.0 / total
+        diag = (diag * inv).astype(BF16)
+        if p:
+            r.PT1[j, pl.ds(0, HP)] = (full * inv).astype(BF16)
+            r.PT1[j, pl.ds(HP, HP)] = diag
+            ot = nn(r.VT[j], r.PT1[j])
+        else:
+            r.PT0[j] = diag
+            ot = nn(r.VT[j, :, pl.ds(0, HP)], diag)
+        r.OT[j, :, rows_of(p)] = ot
+        r.OB[rows_of(p), HD * j : HD * (j + 1)] = ot.T.astype(BF16)
+
+    def to_sibling(st, p, value):
+        r.PF[p] = value.reshape(2, T, D)
+        r.ES[st, p] = r.PF[p, 1 - c].astype(BF16)
+        send(lambda: copy(r.ES.at[st, p], r.ER.at[st, p], r.s_e.at[st, p], r.r_e.at[st, p], sib))
+
+    def chip_sum(st, p):
+        arrive(lambda: copy(r.ES.at[st, p], r.ER.at[st, p], r.s_e.at[st, p], r.r_e.at[st, p], sib))
+        return r.PF[p, c] + r.ER[st, p].astype(F32)
+
+    def xslot(st, p):
+        return 2 * st + p if st < 2 else st + 2
+
+    def xcopy(st, p):
+        i = xslot(st, p)
+        return copy(r.XS.at[i], r.XR.at[i], r.s_x.at[i], r.r_x.at[i], xp)
+
+    def to_x(st, p):
+        r.XS[xslot(st, p)] = chip_sum(st, p).astype(BF16)
+        send(lambda: xcopy(st, p))
+
+    def pair_sum(st, p):
+        arrive(lambda: xcopy(st, p))
+        return r.XS[xslot(st, p)].astype(F32) + r.XR[xslot(st, p)].astype(F32)
+
+    def share(name, st, p):
+        mk = lambda i: copy(name.at[i], name.at[i], r.s_h.at[st, p], r.r_h.at[st, p], sib)
+        send(lambda: mk(2 * p + c))
+        return lambda: arrive(lambda: mk(2 * p + (1 - c)))
+
+    def out_proj(p):
+        to_sibling(0, p, nn(r.OB[rows_of(p)], W2[:, :, pl.ds(0, D)].reshape(HW, D)))
+
+    for j in range(NH):
+        attend(0, j)
+    g_out[2]()
+    out_proj(0)
+    for d in range(3, nz):
+        g_dn[1](d)
+    attend(1, 0)
+    attend(1, 1)
+    to_x(0, 0)
+    attend(1, 2)
+    attend(1, 3)
+    out_proj(1)
+
+    r.SGA[...] = jnp.zeros_like(r.SGA)
+
+    def middle(p):
+        mid = r.X[2 * p + c].astype(F32) + pair_sum(0, p)
+        r.MID[p] = mid
+        inv = lax.rsqrt(jnp.mean(mid * mid, axis=1, keepdims=True) + epsilon)
+        r.HN2[2 * p + c] = (mid * inv * gain_ffn).astype(BF16)
+        return share(r.HN2, 0, p)
+
+    def w_up():
+        return W1[:, :, :, pl.ds(0, HW)].reshape(D, HW)
+
+    def feed(p):
+        hn = r.HN2[pl.ds(2 * p, 2)].reshape(HP, D)
+        u = nn(hn, w_up()) + bias_up
+        sig = 1.0 / (1.0 + jnp.exp(-u))
+        r.ACT[rows_of(p)] = (u * sig).astype(BF16)
+        dy = r.DY[pl.ds(2 * p, 2)].reshape(HP, D)
+        dact = nt(dy, W2[:, :, pl.ds(D, D)].reshape(HW, D))
+        dup = (dact * sig * (1.0 + u * (1.0 - sig))).astype(BF16)
+        r.DUP[rows_of(p), 0:HW] = dup
+        to_sibling(1, p, nt(dup, w_up()))
+        row = pl.ds(4 + s, 1)
+        r.SGA[row, 0:HW] = r.SGA[row, 0:HW] + jnp.sum(dup.astype(F32), axis=0, keepdims=True)
+
+    def transpose_hn2(p):
+        for k in range(2):
+            t = r.HN2[2 * p + k].astype(F32).T.astype(BF16)
+            r.HN2T[:, :, pl.ds((2 * p + k) * T, T)] = t.reshape(2 * nz, 2 * CB, T)
+
+    r.DUP[:, 256:384] = jnp.zeros((L, 128), BF16)
+    r.DQ[:, 0:128] = jnp.zeros((L, 128), BF16)
+    wait_hn = middle(0)
+    to_x(0, 1)
+    g_up[2]()
+    g_dn[2]()
+    wait_hn()
+    feed(0)
+    transpose_hn2(0)
+    wait_hn = middle(1)
+    to_x(1, 0)
+    wait_hn()
+    feed(1)
+    transpose_hn2(1)
+    to_x(1, 1)
+
+    def scatter_item(idx, part, yr, zu, zd, zcond):
+        yc = lambda zz: copy(part(zz, 1 - y), yr(zz), r.s_ry.at[idx, zz], r.r_ry.at[idx, zz], yp)
+        up = lambda zz: copy(part(zz, y), zu(zz), r.s_ru.at[idx, zz], r.r_ru.at[idx, zz], zup)
+        dn = lambda zz: copy(part(zz, y), zd(zz), r.s_rd.at[idx, zz], r.r_rd.at[idx, zz], zdn)
+
+        def add(zz, other):
+            part(zz, y)[...] = (part(zz, y)[...].astype(F32) + other(zz)[...].astype(F32)).astype(BF16)
+
+        def order(visit):
+            for d in range(nz - 1, 0, -1):
+                visit(z + d, z + d < nz)
+                visit(z - d, z - d >= 0)
+            visit(z, None)
+
+        ycond = None if zcond is None else jnp.logical_not(zcond)
+
+        def start():
+            order(lambda zz, ok: send(lambda: yc(zz), both(ok, ycond)))
+
+        def step(d):
+            if d:
+                ok = both(zcond, z + d < nz)
+                from_below = both(ok, z > 0)
+                arrive(lambda: yc(z + d), ok)
+                when(ok, lambda: add(z + d, yr))
+                arrive(lambda: up(z + d), from_below)
+                when(from_below, lambda: add(z + d, zu))
+                send(lambda: up(z + d), ok)
+                ok2 = both(zcond, z - d >= 0)
+                from_above = both(ok2, z < nz - 1)
+                arrive(lambda: yc(z - d), ok2)
+                when(ok2, lambda: add(z - d, yr))
+                arrive(lambda: dn(z - d), from_above)
+                when(from_above, lambda: add(z - d, zd))
+                send(lambda: dn(z - d), ok2)
+            else:
+                arrive(lambda: yc(z), zcond)
+                when(zcond, lambda: add(z, yr))
+                below, above = both(zcond, z > 0), both(zcond, z < nz - 1)
+                arrive(lambda: up(z), below)
+                when(below, lambda: add(z, zu))
+                arrive(lambda: dn(z), above)
+                when(above, lambda: add(z, zd))
+
+        return start, step
+
+    def w1_item(idx, lo, width):
+        cut = pl.ds(lo, width)
+        return scatter_item(
+            idx,
+            lambda zz, q: r.G1.at[2 * zz + q, :, :, cut],
+            lambda zz: r.YR1.at[zz, :, :, cut],
+            lambda zz: r.ZU1.at[zz - 1, :, :, cut],
+            lambda zz: r.ZD1.at[zz, :, :, cut],
+            None,
+        )
+
+    def w2_item(idx, lo, width):
+        cut = pl.ds(lo, width)
+        return scatter_item(
+            idx,
+            lambda zz, q: r.G2.at[zz, :, cut],
+            lambda zz: r.YR2.at[zz, :, cut],
+            lambda zz: r.ZU2.at[zz - 1, :, cut],
+            lambda zz: r.ZD2.at[zz, :, cut],
+            mine,
+        )
+
+    s_up = w1_item(0, 0, LO)
+    s_dn = w2_item(1, D, D)
+    s_out = w2_item(2, 0, D)
+    s_qkv = w1_item(3, LO, D - LO)
+
+    gu = nn(r.HN2T[...].reshape(D, L), r.DUP[...])
+    r.G1[:, :, :, 0:384] = gu.astype(BF16).reshape(2 * nz, 2, CB, 384)
+    s_up[0]()
+    dy_all = r.DY[...].reshape(L, D)
+    r.G2[:, :, pl.ds(D, D)] = tn(r.ACT[...], dy_all).astype(BF16).reshape(nz, CB, D)
+    s_dn[0]()
+
+    def back_middle(p):
+        dh = pair_sum(1, p)
+        mid = r.MID[p]
+        inv = lax.rsqrt(jnp.mean(mid * mid, axis=1, keepdims=True) + epsilon)
+        n = mid * inv
+        dn = dh * gain_ffn
+        dmid = r.DY[2 * p + c].astype(F32) + inv * (
+            dn - n * jnp.mean(dn * n, axis=1, keepdims=True)
+        )
+        r.DMID[p] = dmid
+        r.DA[2 * p + c] = dmid.astype(BF16)
+        own = jnp.where(x == p, jnp.sum(dh * n, axis=0, keepdims=True), 0.0)
+        r.SGA[1:2] = r.SGA[1:2] + own
+        return share(r.DA, 1, p)
+
+    def back_out(p):
+        da = r.DA[pl.ds(2 * p, 2)].reshape(HP, D)
+        r.QKV[0:HP, 0:HW] = nt(da, W2[:, :, pl.ds(0, D)].reshape(HW, D))
+
+    def back_attend(p, j):
+        do = r.QKV[0:HP, HD * j : HD * (j + 1)].astype(BF16)
+        dof = do.astype(F32)
+        delta = jnp.sum(dof.T * r.OT[j, :, rows_of(p)], axis=0, keepdims=True)
+        span = HP * (p + 1)
+        pt = r.PT1[j] if p else r.PT0[j]
+        dpt = nt(r.VH[j, pl.ds(0, span)], do)
+        dst = (pt.astype(F32) * (dpt - delta)).astype(BF16)
+        dv = nn(pt, do)
+        dk = nn(dst, r.QH[j, rows_of(p)])
+        dq = nn(r.KT[j, :, pl.ds(0, span)], dst).T
+        raw = r.QRAW[j, rows_of(p)]
+        r.SGA[3:4, 0:HD] = r.SGA[3:4, 0:HD] + jnp.sum(dq * raw, axis=0, keepdims=True)
+        r.DQ[rows_of(p), off + HD * j : off + HD * (j + 1)] = (dq * factor[:, :HD]).astype(BF16)
+        ko, vo = off + HW + HD * j, off + 2 * HW + HD * j
+        if p == 0:
+            r.DKA[j] = dk
+            r.DVA[j] = dv
+        else:
+            r.DQ[0:HP, ko : ko + HD] = (dk[:HP] + r.DKA[j]).astype(BF16)
+            r.DQ[HP:L, ko : ko + HD] = dk[HP:].astype(BF16)
+            r.DQ[0:HP, vo : vo + HD] = (dv[:HP] + r.DVA[j]).astype(BF16)
+            r.DQ[HP:L, vo : vo + HD] = dv[HP:].astype(BF16)
+
+    def down_proj(p):
+        to_sibling(2, p, nn(r.ACT[rows_of(p)], W2[:, :, pl.ds(D, D)].reshape(HW, D)))
+
+    wait_da = back_middle(0)
+    down_proj(0)
+    down_proj(1)
+    for d in range(nz - 1, 0, -1):
+        s_up[1](d)
+    wait_da()
+    back_out(0)
+    for j in range(NH):
+        back_attend(0, j)
+    for d in range(nz - 1, 0, -1):
+        s_dn[1](d)
+    wait_da = back_middle(1)
+    r.XS[4] = chip_sum(2, 1 - x).astype(BF16)
+    send(lambda: xcopy(2, 0))
+    r.PF2[...] = chip_sum(2, x)
+    wait_da()
+    back_out(1)
+    da_all = r.DA[...].reshape(L, D)
+    r.G2[:, :, pl.ds(0, D)] = tn(r.OB[...], da_all).astype(BF16).reshape(nz, CB, D)
+    s_out[0]()
+    for j in range(NH):
+        back_attend(1, j)
+    s_up[1](0)
+    s_dn[1](0)
+
+    def qkv_block(bb):
+        t = nn(r.HN1T[bb], r.DQ[...]).reshape(2, CB, D - LO)
+        head = t[:, :, 0:128] + r.G1[bb, :, :, pl.ds(LO, 128)].astype(F32)
+        r.G1[bb, :, :, pl.ds(LO, 128)] = head.astype(BF16)
+        r.G1[bb, :, :, pl.ds(384, D - 384)] = t[:, :, 128:].astype(BF16)
+
+    for k in range(nz):
+        qkv_block(2 * k + (1 - y))
+    s_qkv[0]()
+    for k in range(nz):
+        qkv_block(2 * k + y)
+    for d in range(nz - 1, 0, -1):
+        s_out[1](d)
+
+    arrive(lambda: xcopy(2, 0))
+    own_out = r.PF2[...] + r.XR[4].astype(F32)
+    mixed_o[...] = (r.MID[x] + own_out + bias_down).astype(BF16)
+
+    for p in range(2):
+        w = W1[:, :, :, pl.ds(LO, D - LO)].reshape(D, D - LO)
+        to_sibling(3, p, nt(r.DQ[rows_of(p)], w))
+    r.XS[5] = chip_sum(3, 1 - x).astype(BF16)
+    send(lambda: xcopy(3, 0))
+    r.PF2[...] = chip_sum(3, x)
+
+    s_qkv[1](nz - 1)
+    s_out[1](0)
+
+    arrive(lambda: xcopy(3, 0))
+    dh = r.PF2[...] + r.XR[5].astype(F32)
+    xv = r.X[s].astype(F32)
+    inv = lax.rsqrt(jnp.mean(xv * xv, axis=1, keepdims=True) + epsilon)
+    n = xv * inv
+    dn = dh * gain_attn
+    gtok_o[...] = r.DMID[x] + inv * (dn - n * jnp.mean(dn * n, axis=1, keepdims=True))
+    r.SGA[0:1] = jnp.sum(dh * n, axis=0, keepdims=True)
+    r.SGA[2:3] = jnp.sum(r.DY[s].astype(F32), axis=0, keepdims=True)
+
+    def small_copy(k, slot, dev):
+        return lambda: copy(r.SGA if k == 0 else r.SGS.at[k - 1], r.SGR.at[slot], r.s_sg.at[slot], r.r_sg.at[slot], dev)
+
+    total = r.SGA[...]
+    for k, dev in enumerate((sib, xp, yp)):
+        mk = small_copy(k, k, dev)
+        send(mk)
+        if k == 1:
+            for d in range(nz - 2, 0, -1):
+                s_qkv[1](d)
+        arrive(mk)
+        total = total + r.SGR[k]
+        r.SGS[k] = total
+    mks = []
+    for k in range(1, nz):
+        mk = small_copy(3, 2 + k, (2 * lax.rem(z + k, nz) + y, s))
+        send(mk)
+        mks.append(mk)
+    s_qkv[1](0)
+
+    m_fx = lambda: copy(r.G1.at[b, 1 - x], r.FX, r.s_one.at[11], r.r_one.at[11], xp)
+    send(m_fx)
+    done2 = r.G2[z].astype(F32)
+    r.GF2[0] = done2[:RW]
+    r.GF2[1] = done2[RW:]
+    m_g2 = lambda: copy(r.GF2.at[1 - c], r.GR2, r.s_one.at[12], r.r_one.at[12], sib)
+    send(m_g2, mine)
+    own = r.G1[b, x].astype(F32)
+    r.GF[0, x] = own[:RW]
+    r.GF[1, x] = own[RW:]
+    for k, mk in enumerate(mks):
+        arrive(mk)
+        total = total + r.SGR[3 + k]
+    sg_o[...] = total
+    not_mine = jnp.logical_not(mine)
+    arrive(m_g2, not_mine)
+
+    def out2_own():
+        o2[...] = r.GF2[c]
+
+    def out2_sib():
+        o2[...] = r.GR2[...]
+
+    when(mine, out2_own)
+    when(not_mine, out2_sib)
+    arrive(m_fx)
+    other = r.FX[...].astype(F32)
+    r.GF[0, 1 - x] = other[:RW]
+    r.GF[1, 1 - x] = other[RW:]
+    m_gf = lambda: copy(r.GF.at[1 - c], r.GRV, r.s_one.at[13], r.r_one.at[13], sib)
+    send(m_gf)
+    o1[:, c] = r.GF[c]
+    arrive(m_gf)
+    o1[:, 1 - c] = r.GRV[...]
+
+    for make, cond in drains:
+        when(cond, lambda make=make: make().wait_send())
+
+
+def fused_layer(nb, ns, tokens, wqkv, wout, wup, wdown, gattn, gffn, bup, bdown, scale_param, cot):
+    nz = nb // 2
+    rows, D = wout.shape
+    T = tokens.shape[1]
+    L = ns * T
+    cols = jnp.concatenate([wup.reshape(rows, 1, 4, 2, 2, HD), wqkv.reshape(rows, 3, 4, 2, 2, HD)], axis=1)
+    w1p = jnp.transpose(cols, (3, 4, 0, 1, 2, 5)).reshape(2, 2, rows, D)
+    w1p = jnp.pad(w1p, ((0, 0), (0, 0), (0, 8), (0, 0)))
+    w2p = jnp.pad(jnp.concatenate([wout, wdown], axis=1), ((0, 8), (0, 0)))
+    smalls = jnp.stack([gattn, gffn, bup, bdown]).astype(F32)
+    smalls = jnp.pad(smalls, ((0, 4), (0, 128 - rows)))
+    scale = jnp.broadcast_to(jnp.tile(scale_param.astype(F32), 4)[None], (8, 4 * HD))
+    V = pltpu.VMEM
+    scratch = dict(
+        SIB1=V((2, 48, D), BF16),
+        SIB2=V((48, 2 * D), BF16),
+        CB1=V((HD, D), BF16),
+        W1=V((nb, 2, HD, D), BF16),
+        W2=V((nz, HD, 2 * D), BF16),
+        S=V((nb, 4, 8, 128), F32),
+        X=V((4, T, D), BF16),
+        DY=V((4, T, D), BF16),
+        ROWS=V((8, D), F32),
+        BUP=V((8, 4 * HD), F32),
+        HN1=V((L, D), BF16),
+        HN1T=V((nb, 2 * HD, L), BF16),
+        HN2T=V((nb, 2 * HD, L), BF16),
+        QKV=V((L, D - 256), F32),
+        QRAW=V((4, L, HD), F32),
+        QH=V((4, L, HD), BF16),
+        KH=V((4, L, HD), BF16),
+        VH=V((4, L, HD), BF16),
+        KT=V((4, HD, L), BF16),
+        VT=V((4, HD, L), BF16),
+        PT0=V((4, L // 2, L // 2), BF16),
+        PT1=V((4, L, L // 2), BF16),
+        OT=V((4, HD, L), F32),
+        OB=V((L, 4 * HD), BF16),
+        PF=V((2, 2, T, D), F32),
+        PF2=V((T, D), F32),
+        ES=V((4, 2, T, D), BF16),
+        ER=V((4, 2, T, D), BF16),
+        XS=V((6, T, D), BF16),
+        XR=V((6, T, D), BF16),
+        MID=V((2, T, D), F32),
+        HN2=V((4, T, D), BF16),
+        ACT=V((L, 4 * HD), BF16),
+        DUP=V((L, 384), BF16),
+        DA=V((4, T, D), BF16),
+        DMID=V((2, T, D), F32),
+        DQ=V((L, D - 256), BF16),
+        DKA=V((4, L // 2, HD), F32),
+        DVA=V((4, L // 2, HD), F32),
+        G1=V((nb, 2, HD, D), BF16),
+        G2=V((nz, HD, 2 * D), BF16),
+        YR1=V((nz, 2, HD, D), BF16),
+        ZU1=V((nz - 1, 2, HD, D), BF16),
+        ZD1=V((nz - 1, 2, HD, D), BF16),
+        YR2=V((nz, HD, 2 * D), BF16),
+        ZU2=V((nz - 1, HD, 2 * D), BF16),
+        ZD2=V((nz - 1, HD, 2 * D), BF16),
+        FX=V((HD, D), BF16),
+        GF=V((2, 2, rows, D), F32),
+        GRV=V((2, rows, D), F32),
+        GF2=V((2, rows, 2 * D), F32),
+        GR2=V((rows, 2 * D), F32),
+        SGA=V((8, D), F32),
+        SGS=V((3, 8, D), F32),
+        SGR=V((2 + nz, 8, D), F32),
+    )
+    dma = pltpu.SemaphoreType.DMA
+    scratch.update(
+        s_one=dma((14,)), r_one=dma((14,)),
+        s_up=dma((5, nz)), r_up=dma((5, nz)),
+        s_dn=dma((5, nz)), r_dn=dma((5, nz)),
+        s_y=dma((5, nz)), r_y=dma((5, nz)),
+        s_e=dma((4, 2)), r_e=dma((4, 2)),
+        s_x=dma((6,)), r_x=dma((6,)),
+        s_h=dma((2, 2)), r_h=dma((2, 2)),
+        s_ry=dma((4, nz)), r_ry=dma((4, nz)),
+        s_ru=dma((4, nz)), r_ru=dma((4, nz)),
+        s_rd=dma((4, nz)), r_rd=dma((4, nz)),
+        s_sg=dma((2 + nz,)), r_sg=dma((2 + nz,)),
+    )
+    vmem = pl.BlockSpec(memory_space=pltpu.VMEM)
+    mixed, gtok, o1, o2, sg = pl.pallas_call(
+        functools.partial(layer_kernel, nz, tuple(scratch)),
+        out_shape=(
+            jax.ShapeDtypeStruct((T, D), BF16),
+            jax.ShapeDtypeStruct((T, D), F32),
+            jax.ShapeDtypeStruct((2, 2, rows, D), F32),
+            jax.ShapeDtypeStruct((rows, 2 * D), F32),
+            jax.ShapeDtypeStruct((8, D), F32),
+        ),
+        in_specs=[vmem] * 6,
+        out_specs=(vmem,) * 5,
+        scratch_shapes=list(scratch.values()),
+        compiler_params=pltpu.CompilerParams(
+            collective_id=0, has_side_effects=True, vmem_limit_bytes=63 << 20
+        ),
+        name="decoder_layer",
+    )(tokens[0], cot[0], w1p, w2p, smalls, scale)
+    grads = jnp.transpose(o1.reshape(2, 2, rows, 4, 4, HD), (2, 3, 4, 1, 0, 5)).reshape(rows, 4 * D)
+    b, s = lax.axis_index("batch"), lax.axis_index("seq")
+    at = (b * ns + s) * rows
+    own = lambda v: lax.dynamic_slice(v, (at,), (rows,))
+    bias_up = jnp.transpose(sg[4:8, : 4 * HD].reshape(2, 2, 4, HD), (2, 1, 0, 3)).reshape(D)
+    scale_float = scale_param.astype(F32)
+    grad_scale = sg[3, :HD] * (soft_unit / math.sqrt(HD)) * jax.nn.sigmoid(scale_float)
+    return (
+        mixed[None],
+        gtok[None],
+        grads[:, D:],
+        o2[:, :D],
+        grads[:, :D],
+        o2[:, D:],
+        own(sg[0]),
+        own(sg[1]),
+        own(bias_up),
+        own(sg[2]),
+        grad_scale,
+    )
+
+
+def layer_step(nb, ns, *args):
+    if fits_fused(nb, ns, args[0], args[1], args[3]):
+        return fused_layer(nb, ns, *args)
+    return generic_layer(*args)
+
+
 def solution(mesh):
     return jax.shard_map(
-        body,
+        functools.partial(layer_step, mesh.shape["batch"], mesh.shape["seq"]),
         mesh=mesh,
         in_specs=(
             P("batch", "seq", None),

time: 1070 us -> 198 us (0.19)
  waiting for transfers between devices: 829 us -> 0 us
  Pallas kernels: 0 us -> 173 us
  blocking collectives: 85 us -> 0 us
  matrix products: 68.9 us -> 0 us
  local copies, waits for them, and re-layouts: 56.2 us -> 18.1 us
  between operations: 14.2 us -> 0.77 us
    reduce_scatter x4 -> x0, waiting for transfers between devices: 582 us -> none  [the longest x1 216 us: body(): lax.psum_scatter(grad_qkv, ('batch', 'seq'), scatter_dimension=0, tiled=T...]
    all_gather x6 -> x0, waiting for transfers between devices: 229 us -> none  [the longest x1 58.2 us: body(): lax.all_gather(shards[2], ('batch', 'seq'), axis=0, tiled=True)]
    pallas_call x0 -> x1, Pallas kernels: none -> 173 us  [fused_layer(): pl.pallas_call(functools.partial(layer_kernel, nz, tuple(scratch)), out_s...]
    unnamed x2 -> x0, blocking collectives: 85 us -> none
    dot_general x40 -> x0, matrix products: 68.9 us -> none  [the longest x1 8.28 us: body(): jnp.einsum('rd,re->de', attention_normed_input, grad_qkv_low, preferred_e...]
    unnamed x80 -> x12, local copies, waits for them, and re-layouts: 35.6 us -> 1.58 us
    unnamed x12 -> x0, waiting for transfers between devices: 18.3 us -> none
    dynamic_slice x12 -> x3, local copies, waits for them, and re-layouts: 13.1 us -> 1.77 us  [fused_layer(): own = lambda v: lax.dynamic_slice(v, (at,), (rows,))]
  transfers between devices with their start and end apart: 11 -> 0, of which waited for: 11 -> 0; matrix products, arithmetic and copies ran while one was open for 7% -> 0% of each run, Pallas kernels for 0% -> 0%
where the time goes in v1:
time: 198 us; the launch traced here: 197 us
  Pallas kernels  173 us (87%)
  local copies, waits for them, and re-layouts  18.1 us (9%)
  other arithmetic  4.78 us (2%)
    pallas_call x1, Pallas kernels, fused_layer(): pl.pallas_call(functools.partial(layer_kernel, nz, tuple(scratch)), out_s...  173 us

profile of v1, /device:TPU:0, one launch (start us, length us, event | category | flops | bytes accessed | tf_op | source)
XLA Modules:
  0.0 196.8 jit_solution(4224772468284748585)
XLA Ops:
  0.7 0.7 tile.2
  1.4 1.3 fusion.12.smalls
  2.8 0.6 broadcast_in_dim.14.scl
  3.4 1.1 reshape.50
  4.6 1.7 fusion.2.w2p
  6.2 0.8 reshape.51
  7.2 0.5 maximum_bitcast_fusion
  7.8 0.6 reshape.52
  8.5 0.8 pad.14.w1p
  9.3 173.1 %decoder_layer.1 = (bf16[128,1280]{1,0:T(8,128)(2,1)}, f32[128,1280]{1,0:T(8,128)}, f32[2,2,40,1280]{3,2,1,0:T(8,128)}, f32[40,2560]{1,0:T(8,128)}, f32[8,1280]{1,0:T(8,128)}) custom-call(bf16[128,1280]{1,0:T(8,128)(2,1)} %bitcast.27, bf16[128,1280]{1,0:T(8,128)(2,1)} %bitcast.28, bf16[2,2,48,1280]{3,2,1,0:T(8,128)(2,1)} %pad.14.w1p, ...), custom_call_target="tpu_custom_call" | custom-call | tf_op jit(solution)/shard_map/decoder_layer/pallas_call | solution.py:988
  182.4 1.3 divide_multiply_fusion
  183.7 0.7 slice.33
  184.4 0.9 fusion.20
  185.3 0.6 fusion.18
  185.9 0.6 fusion.16
  186.7 0.6 dynamic_slice.22
  187.3 1.8 fusion.19
  189.1 1.7 reshape.53
  190.8 1.0 copy.27
  191.8 1.9 reshape.54
  193.7 0.7 slice.37
  194.4 0.9 slice.36
  195.2 0.7 copy.33
  196.0 0.8 copy.34
  (16 shorter events, 0.5 us)
Async XLA Ops:
  0.6 5.6 %copy-start.3 = (bf16[40,3840]{1,0:T(8,128)(2,1)S(1)}, bf16[40,3840]{1,0:T(8,128)(2,1)}, u32[]{:S(2)}) copy-start(bf16[40,3840]{1,0:T(8,128)(2,1)} %param.12) | copy-start | bytes 921604
  8.4 174.0 %copy-start.4 = (bf16[80]{0:T(256)(128)(2,1)S(1)}, bf16[80]{0:T(256)(128)(2,1)}, u32[]{:S(2)}) copy-start(bf16[80]{0:T(256)(128)(2,1)} %param.20) | copy-start | bytes 484
  182.4 6.7 %copy-start = (f32[2,2,40,1280]{3,2,1,0:T(8,128)S(1)}, f32[2,2,40,1280]{3,2,1,0:T(8,128)}, u32[]{:S(2)}) copy-start(f32[2,2,40,1280]{3,2,1,0:T(8,128)} %get-tuple-element.18) | copy-start | bytes 2457604
  193.7 1.6 copy-start.2
  193.7 2.3 %copy-start.1 = (f32[128,1280]{1,0:T(8,128)S(1)}, f32[128,1280]{1,0:T(8,128)}, u32[]{:S(2)}) copy-start(f32[128,1280]{1,0:T(8,128)} %get-tuple-element.17) | copy-start | bytes 1966084

commit v2 on v1

--- a/solution.py
+++ b/solution.py
@@ -297,7 +297,7 @@
     return lax.dot_general(a, b, (((0,), (0,)), ((), ())), preferred_element_type=F32)
 
 
-def layer_kernel(nz, scratch_names, tok, cot, w1p, w2p, smalls, scl, *refs):
+def layer_kernel(nz, scratch_names, tok, cot, wqkv, wout, wup, wdown, ga, gf, bu, bd, scl, *refs):
     mixed_o, gtok_o, o1, o2, sg_o = refs[:5]
     r = types.SimpleNamespace(**dict(zip(scratch_names, refs[5:])))
     D = tok.shape[1]
@@ -351,17 +351,51 @@
         peers.append((2 * lax.rem(z + k, nz) + y, s))
     for dev in peers:
         pl.semaphore_signal(bar, inc=1, device_id=dev, device_id_type=MESH)
+    fetches = [
+        pltpu.make_async_copy(src, dst, r.s_in.at[k])
+        for k, (src, dst) in enumerate(
+            (
+                (wqkv, r.WQ),
+                (wup, r.WU),
+                (wout, r.WO),
+                (wdown, r.WD),
+                (tok, r.X.at[s]),
+                (cot, r.DY.at[s]),
+            )
+        )
+    ]
+    for f in fetches:
+        f.start()
+    small_rows = [v[...].astype(F32).reshape(1, RW) for v in (ga, gf, bu, bd)]
+    r.SM[...] = jnp.zeros_like(r.SM)
+    for k, row in enumerate(small_rows):
+        r.SM[k : k + 1, 0:RW] = row
+    fetches[0].wait()
+    fetches[1].wait()
+
+    def pieces(cc):
+        for xx in range(2):
+            for t in range(4):
+                for j in range(NH):
+                    src = HD * (4 * j + 2 * cc + xx)
+                    v = r.WU[:, src : src + HD] if t == 0 else r.WQ[:, D * (t - 1) + src : D * (t - 1) + src + HD]
+                    r.W1P[cc, xx, 0:RW, HW * t + HD * j : HW * t + HD * (j + 1)] = v
+
+    pieces(0)
+    pieces(1)
     pl.semaphore_wait(bar, len(peers))
 
-    m_sib1 = lambda: copy(w1p.at[1 - c], r.SIB1, r.s_one.at[0], r.r_one.at[0], sib)
-    m_ssib = lambda: copy(smalls, r.S.at[b, s], r.s_one.at[1], r.r_one.at[1], sib)
-    m_sib2 = lambda: copy(w2p, r.SIB2, r.s_one.at[2], r.r_one.at[2], sib)
+    m_sib1 = lambda: copy(r.W1P.at[1 - c], r.SIB1, r.s_one.at[0], r.r_one.at[0], sib)
+    m_ssib = lambda: copy(r.SM, r.S.at[b, s], r.s_one.at[1], r.r_one.at[1], sib)
+    m_sib2 = lambda: copy(r.W2P, r.SIB2, r.s_one.at[2], r.r_one.at[2], sib)
     send(m_sib1)
     send(m_ssib)
+    fetches[2].wait()
+    fetches[3].wait()
+    r.W2P[0:RW, 0:D] = r.WO[...]
+    r.W2P[0:RW, D : 2 * D] = r.WD[...]
     send(m_sib2)
-    r.S[b, s] = smalls[...]
-    r.X[s] = tok[...]
-    r.DY[s] = cot[...]
+    r.S[b, s] = r.SM[...]
 
     def chip_rows(own, other):
         own, other = own[:RW].astype(F32), other[:RW].astype(F32)
@@ -370,33 +404,11 @@
         return jnp.concatenate([lo, hi], axis=0).astype(BF16)
 
     arrive(m_sib1)
-    r.CB1[...] = chip_rows(w1p[c, 1 - x], r.SIB1[1 - x])
+    r.CB1[...] = chip_rows(r.W1P[c, 1 - x], r.SIB1[1 - x])
     m_x1 = lambda: copy(r.CB1, r.W1.at[b, x], r.s_one.at[3], r.r_one.at[3], xp)
     send(m_x1)
-    r.W1[b, x] = chip_rows(w1p[c, x], r.SIB1[x])
-    m_ssib_r = lambda: copy(smalls, r.S.at[b, 2 * x + (1 - c)], r.s_one.at[1], r.r_one.at[1], sib)
-    arrive(m_ssib_r)
-    m_xs = lambda: copy(
-        r.S.at[b, pl.ds(2 * x, 2)], r.S.at[b, pl.ds(2 * x, 2)], r.s_one.at[4], r.r_one.at[4], xp
-    )
-    send(m_xs)
-    m_xt = lambda: copy(tok, r.X.at[s], r.s_one.at[5], r.r_one.at[5], xp)
-    m_st = lambda: copy(tok, r.X.at[s], r.s_one.at[6], r.r_one.at[6], sib)
-    m_xc = lambda: copy(cot, r.DY.at[s], r.s_one.at[7], r.r_one.at[7], xp)
-    m_sc = lambda: copy(cot, r.DY.at[s], r.s_one.at[8], r.r_one.at[8], sib)
-    send(m_xt)
-    send(m_st)
-    send(m_xc)
-    send(m_sc)
-    arrive(m_sib2)
-
-    def fill_w2():
-        r.W2[z] = chip_rows(w2p[...], r.SIB2[...])
-
-    mine = c == y
-    when(mine, fill_w2)
-
-    def gather_item(idx, block, zcond):
+    r.W1[b, x] = chip_rows(r.W1P[c, x], r.SIB1[x])
+    def gather_item(idx, block, zcond, passes_y=True):
         up = lambda zz: copy(block(zz, y), block(zz, y), r.s_up.at[idx, zz], r.r_up.at[idx, zz], zup)
         dn = lambda zz: copy(block(zz, y), block(zz, y), r.s_dn.at[idx, zz], r.r_dn.at[idx, zz], zdn)
         yy = lambda zz: copy(block(zz, y), block(zz, y), r.s_y.at[idx, zz], r.r_y.at[idx, zz], yp)
@@ -404,7 +416,8 @@
         def start():
             send(lambda: up(z), both(zcond, z < nz - 1))
             send(lambda: dn(z), both(zcond, z > 0))
-            send(lambda: yy(z), zcond)
+            if passes_y:
+                send(lambda: yy(z), zcond)
 
         def step(d):
             lo, hi = z - d, z + d
@@ -413,25 +426,58 @@
             send(lambda: up(lo), both(below, z < nz - 1))
             arrive(lambda: dn(hi), above)
             send(lambda: dn(hi), both(above, z > 0))
-            send(lambda: yy(lo), below)
-            send(lambda: yy(hi), above)
+            if passes_y:
+                send(lambda: yy(lo), below)
+                send(lambda: yy(hi), above)
 
         def finish():
-            for k in range(nz):
-                when(
-                    None if zcond is None else jnp.logical_not(zcond),
-                    lambda k=k: copy(
-                        block(k, 1 - y), block(k, 1 - y), r.s_y.at[idx, k], r.r_y.at[idx, k], yp
-                    ).wait_recv(),
-                )
+            if passes_y:
+                for k in range(nz):
+                    when(
+                        None if zcond is None else jnp.logical_not(zcond),
+                        lambda k=k: copy(
+                            block(k, 1 - y), block(k, 1 - y), r.s_y.at[idx, k], r.r_y.at[idx, k], yp
+                        ).wait_recv(),
+                    )
 
         return start, step, finish
 
+    mine = c == y
+    not_mine = c != y
     g_s = gather_item(0, lambda zz, q: r.S.at[2 * zz + q], None)
-    g_qkv = gather_item(1, lambda zz, q: r.W1.at[2 * zz + q, :, :, pl.ds(LO, D - LO)], None)
-    g_out = gather_item(2, lambda zz, q: r.W2.at[zz, :, pl.ds(0, D)], mine)
-    g_up = gather_item(3, lambda zz, q: r.W1.at[2 * zz + q, :, :, pl.ds(0, LO)], None)
-    g_dn = gather_item(4, lambda zz, q: r.W2.at[zz, :, pl.ds(D, D)], mine)
+    g_own = gather_item(1, lambda zz, q: r.W1.at[2 * zz + q, x, :, pl.ds(LO, D - LO)], None)
+    g_oth = gather_item(2, lambda zz, q: r.W1.at[2 * zz + q, 1 - x, :, pl.ds(LO, D - LO)], None)
+    g_out = gather_item(3, lambda zz, q: r.W2.at[zz, :, pl.ds(0, D)], None, False)
+    g_up = gather_item(4, lambda zz, q: r.W1.at[2 * zz + q, :, :, pl.ds(0, LO)], None)
+    g_dn = gather_item(5, lambda zz, q: r.W2.at[zz, :, pl.ds(D, D)], mine)
+
+    g_own[0]()
+    m_ssib_r = lambda: copy(r.SM, r.S.at[b, 2 * x + (1 - c)], r.s_one.at[1], r.r_one.at[1], sib)
+    arrive(m_ssib_r)
+    m_xs = lambda: copy(
+        r.S.at[b, pl.ds(2 * x, 2)], r.S.at[b, pl.ds(2 * x, 2)], r.s_one.at[4], r.r_one.at[4], xp
+    )
+    send(m_xs)
+    fetches[4].wait()
+    fetches[5].wait()
+    own_tok, own_cot = r.X.at[s], r.DY.at[s]
+    m_xt = lambda: copy(own_tok, own_tok, r.s_one.at[5], r.r_one.at[5], xp)
+    m_st = lambda: copy(own_tok, own_tok, r.s_one.at[6], r.r_one.at[6], sib)
+    m_xc = lambda: copy(own_cot, own_cot, r.s_one.at[7], r.r_one.at[7], xp)
+    m_sc = lambda: copy(own_cot, own_cot, r.s_one.at[8], r.r_one.at[8], sib)
+    send(m_xt)
+    send(m_st)
+    send(m_xc)
+    send(m_sc)
+    arrive(m_sib2)
+
+    def fill_w2():
+        r.W2[z] = chip_rows(r.W2P[...], r.SIB2[...])
+
+    when(mine, fill_w2)
+    m_y2 = lambda: copy(
+        r.W2.at[z, :, pl.ds(0, D)], r.W2.at[z, :, pl.ds(0, D)], r.s_one.at[14], r.r_one.at[14], yp
+    )
 
     m_x1_r = lambda: copy(r.CB1, r.W1.at[b, 1 - x], r.s_one.at[3], r.r_one.at[3], xp)
     m_xs_r = lambda: copy(
@@ -441,33 +487,41 @@
         r.r_one.at[4],
         xp,
     )
-    arrive(m_xs_r)
-    arrive(m_x1_r)
-    g_s[0]()
-    g_qkv[0]()
     sx = 2 * (1 - x) + c
     so = 2 * (1 - x) + (1 - c)
     ss = 2 * x + (1 - c)
     fwd = lambda name, k, src_i: copy(
         name.at[src_i], name.at[src_i], r.s_one.at[k], r.r_one.at[k], sib
     )
-    arrive(lambda: copy(tok, r.X.at[sx], r.s_one.at[5], r.r_one.at[5], xp))
+    arrive(m_x1_r)
+    g_oth[0]()
+    arrive(m_xs_r)
+    g_s[0]()
+    send(m_y2, mine)
+    g_own[1](1)
+    arrive(lambda: copy(own_tok, r.X.at[sx], r.s_one.at[5], r.r_one.at[5], xp))
     send(lambda: fwd(r.X, 9, sx))
+    g_oth[1](1)
     g_s[1](1)
-    g_qkv[1](1)
-    arrive(lambda: copy(cot, r.DY.at[sx], r.s_one.at[7], r.r_one.at[7], xp))
+    arrive(m_y2, not_mine)
+    g_out[0]()
+    g_own[1](2)
+    arrive(lambda: copy(own_tok, r.X.at[ss], r.s_one.at[6], r.r_one.at[6], sib))
+    arrive(lambda: fwd(r.X, 9, so))
+    g_oth[1](2)
+    g_s[1](2)
+    arrive(lambda: copy(own_cot, r.DY.at[sx], r.s_one.at[7], r.r_one.at[7], xp))
     send(lambda: fwd(r.DY, 10, sx))
-    arrive(lambda: copy(tok, r.X.at[ss], r.s_one.at[6], r.r_one.at[6], sib))
-    arrive(lambda: fwd(r.X, 9, so))
-    arrive(lambda: copy(cot, r.DY.at[ss], r.s_one.at[8], r.r_one.at[8], sib))
-    arrive(lambda: fwd(r.DY, 10, so))
-    for d in range(2, nz):
+    arrive(lambda: copy(own_cot, r.DY.at[ss], r.s_one.at[8], r.r_one.at[8], sib))
+    for d in range(3, nz):
+        g_own[1](d)
+        g_oth[1](d)
         g_s[1](d)
-        g_qkv[1](d)
-    g_out[0]()
     g_up[0]()
     g_dn[0]()
+    g_out[1](1)
     g_s[2]()
+    arrive(lambda: fwd(r.DY, 10, so))
 
     jf = lax.broadcasted_iota(jnp.int32, (1, D), 1).astype(F32)
     jk = jnp.floor((jf + 0.5) / RW)
@@ -490,7 +544,7 @@
     gain_ffn = r.ROWS[1:2]
     bias_down = r.ROWS[3:4]
     bias_up = r.BUP[2:3]
-    scale = scl[0:1, :]
+    scale = scl[...].astype(F32).reshape(1, HD)
     factor = soft_unit / math.sqrt(HD) * (
         jnp.maximum(scale, 0.0) + jnp.log(1.0 + jnp.exp(-jnp.abs(scale)))
     )
@@ -501,35 +555,28 @@
         hn = xv * inv * gain_attn
         r.HN1[pl.ds(k * T, T)] = hn.astype(BF16)
         r.HN1T[:, :, pl.ds(k * T, T)] = hn.T.astype(BF16).reshape(2 * nz, 2 * CB, T)
-    g_out[1](1)
-    g_qkv[2]()
-    g_up[1](1)
+    g_out[1](2)
+    g_own[2]()
+    g_oth[2]()
+    for d in range(3, nz):
+        g_out[1](d)
 
     W1 = r.W1
     W2 = r.W2
     for h in range(2):
         wq = W1[:, :, :, pl.ds(LO + 512 * h, 512)].reshape(D, 512)
         r.QKV[:, pl.ds(512 * h, 512)] = nn(r.HN1[...], wq)
-    g_out[1](2)
-    g_up[1](2)
-    g_dn[1](1)
     off = HW - LO
     for j in range(NH):
         q = r.QKV[:, off + HD * j : off + HD * (j + 1)]
         k = r.QKV[:, off + HW + HD * j : off + HW + HD * (j + 1)]
         v = r.QKV[:, off + 2 * HW + HD * j : off + 2 * HW + HD * (j + 1)]
         r.QRAW[j] = q
-        r.QH[j] = (q * factor[:, :HD]).astype(BF16)
+        r.QH[j] = (q * factor).astype(BF16)
         r.KH[j] = k.astype(BF16)
         r.VH[j] = v.astype(BF16)
         r.KT[j] = k.T.astype(BF16)
         r.VT[j] = v.T.astype(BF16)
-    for d in range(3, nz):
-        g_out[1](d)
-        g_up[1](d)
-    if nz > 2:
-        g_dn[1](2)
-
     tri_k = lax.broadcasted_iota(jnp.int32, (HP, HP), 0)
     tri_q = lax.broadcasted_iota(jnp.int32, (HP, HP), 1)
     seen = tri_k <= tri_q
@@ -595,16 +642,19 @@
 
     for j in range(NH):
         attend(0, j)
-    g_out[2]()
     out_proj(0)
-    for d in range(3, nz):
-        g_dn[1](d)
+    g_up[1](1)
     attend(1, 0)
     attend(1, 1)
     to_x(0, 0)
+    g_dn[1](1)
     attend(1, 2)
     attend(1, 3)
     out_proj(1)
+    for d in range(2, nz):
+        g_up[1](d)
+        g_dn[1](d)
+    to_x(0, 1)
 
     r.SGA[...] = jnp.zeros_like(r.SGA)
 
@@ -639,7 +689,6 @@
     r.DUP[:, 256:384] = jnp.zeros((L, 128), BF16)
     r.DQ[:, 0:128] = jnp.zeros((L, 128), BF16)
     wait_hn = middle(0)
-    to_x(0, 1)
     g_up[2]()
     g_dn[2]()
     wait_hn()
@@ -652,7 +701,7 @@
     transpose_hn2(1)
     to_x(1, 1)
 
-    def scatter_item(idx, part, yr, zu, zd, zcond):
+    def scatter_item(idx, part, yr, zu, zd, zcond, y_first=True):
         yc = lambda zz: copy(part(zz, 1 - y), yr(zz), r.s_ry.at[idx, zz], r.r_ry.at[idx, zz], yp)
         up = lambda zz: copy(part(zz, y), zu(zz), r.s_ru.at[idx, zz], r.r_ru.at[idx, zz], zup)
         dn = lambda zz: copy(part(zz, y), zd(zz), r.s_rd.at[idx, zz], r.r_rd.at[idx, zz], zdn)
@@ -660,77 +709,91 @@
         def add(zz, other):
             part(zz, y)[...] = (part(zz, y)[...].astype(F32) + other(zz)[...].astype(F32)).astype(BF16)
 
-        def order(visit):
-            for d in range(nz - 1, 0, -1):
-                visit(z + d, z + d < nz)
-                visit(z - d, z - d >= 0)
-            visit(z, None)
-
         ycond = None if zcond is None else jnp.logical_not(zcond)
 
-        def start():
-            order(lambda zz, ok: send(lambda: yc(zz), both(ok, ycond)))
+        def start(d):
+            if d:
+                send(lambda: yc(z + d), both(z + d < nz, ycond))
+                send(lambda: yc(z - d), both(z - d >= 0, ycond))
+            else:
+                send(lambda: yc(z), ycond)
 
         def step(d):
             if d:
                 ok = both(zcond, z + d < nz)
                 from_below = both(ok, z > 0)
-                arrive(lambda: yc(z + d), ok)
-                when(ok, lambda: add(z + d, yr))
+                if y_first:
+                    arrive(lambda: yc(z + d), ok)
+                    when(ok, lambda: add(z + d, yr))
                 arrive(lambda: up(z + d), from_below)
                 when(from_below, lambda: add(z + d, zu))
                 send(lambda: up(z + d), ok)
                 ok2 = both(zcond, z - d >= 0)
                 from_above = both(ok2, z < nz - 1)
-                arrive(lambda: yc(z - d), ok2)
-                when(ok2, lambda: add(z - d, yr))
+                if y_first:
+                    arrive(lambda: yc(z - d), ok2)
+                    when(ok2, lambda: add(z - d, yr))
                 arrive(lambda: dn(z - d), from_above)
                 when(from_above, lambda: add(z - d, zd))
                 send(lambda: dn(z - d), ok2)
             else:
-                arrive(lambda: yc(z), zcond)
-                when(zcond, lambda: add(z, yr))
                 below, above = both(zcond, z > 0), both(zcond, z < nz - 1)
                 arrive(lambda: up(z), below)
                 when(below, lambda: add(z, zu))
                 arrive(lambda: dn(z), above)
                 when(above, lambda: add(z, zd))
+                if y_first:
+                    arrive(lambda: yc(z), zcond)
+                    when(zcond, lambda: add(z, yr))
 
         return start, step
 
-    def w1_item(idx, lo, width):
-        cut = pl.ds(lo, width)
+    far = range(nz - 1, 0, -1)
+    cut_up, cut_qkv = pl.ds(0, LO), pl.ds(LO, D - LO)
+    s_up = scatter_item(
+        0,
+        lambda zz, q: r.G1.at[2 * zz + q, :, :, cut_up],
+        lambda zz: r.YR1.at[zz, :, :, cut_up],
+        lambda zz: r.ZU1.at[zz - 1, :, :, cut_up],
+        lambda zz: r.ZD1.at[zz, :, :, cut_up],
+        None,
+    )
+
+    def qkv_item(idx, xx):
         return scatter_item(
             idx,
-            lambda zz, q: r.G1.at[2 * zz + q, :, :, cut],
-            lambda zz: r.YR1.at[zz, :, :, cut],
-            lambda zz: r.ZU1.at[zz - 1, :, :, cut],
-            lambda zz: r.ZD1.at[zz, :, :, cut],
+            lambda zz, q: r.G1.at[2 * zz + q, xx, :, cut_qkv],
+            lambda zz: r.YR1.at[zz, xx, :, cut_qkv],
+            lambda zz: r.ZU1.at[zz - 1, xx, :, cut_qkv],
+            lambda zz: r.ZD1.at[zz, xx, :, cut_qkv],
             None,
         )
 
-    def w2_item(idx, lo, width):
-        cut = pl.ds(lo, width)
+    def w2_item(idx, lo, zcond, y_first):
+        cut = pl.ds(lo, D)
         return scatter_item(
             idx,
             lambda zz, q: r.G2.at[zz, :, cut],
             lambda zz: r.YR2.at[zz, :, cut],
             lambda zz: r.ZU2.at[zz - 1, :, cut],
             lambda zz: r.ZD2.at[zz, :, cut],
-            mine,
-        )
-
-    s_up = w1_item(0, 0, LO)
-    s_dn = w2_item(1, D, D)
-    s_out = w2_item(2, 0, D)
-    s_qkv = w1_item(3, LO, D - LO)
+            zcond,
+            y_first,
+        )
+
+    s_dn = w2_item(1, D, mine, True)
+    s_out = w2_item(2, 0, None, False)
+    s_far = qkv_item(3, 1 - x)
+    s_own = qkv_item(4, x)
 
     gu = nn(r.HN2T[...].reshape(D, L), r.DUP[...])
     r.G1[:, :, :, 0:384] = gu.astype(BF16).reshape(2 * nz, 2, CB, 384)
-    s_up[0]()
+    for d in (*far, 0):
+        s_up[0](d)
     dy_all = r.DY[...].reshape(L, D)
     r.G2[:, :, pl.ds(D, D)] = tn(r.ACT[...], dy_all).astype(BF16).reshape(nz, CB, D)
-    s_dn[0]()
+    for d in (*far, 0):
+        s_dn[0](d)
 
     def back_middle(p):
         dh = pair_sum(1, p)
@@ -764,7 +827,7 @@
         dq = nn(r.KT[j, :, pl.ds(0, span)], dst).T
         raw = r.QRAW[j, rows_of(p)]
         r.SGA[3:4, 0:HD] = r.SGA[3:4, 0:HD] + jnp.sum(dq * raw, axis=0, keepdims=True)
-        r.DQ[rows_of(p), off + HD * j : off + HD * (j + 1)] = (dq * factor[:, :HD]).astype(BF16)
+        r.DQ[rows_of(p), off + HD * j : off + HD * (j + 1)] = (dq * factor).astype(BF16)
         ko, vo = off + HW + HD * j, off + 2 * HW + HD * j
         if p == 0:
             r.DKA[j] = dk
@@ -781,27 +844,28 @@
     wait_da = back_middle(0)
     down_proj(0)
     down_proj(1)
-    for d in range(nz - 1, 0, -1):
-        s_up[1](d)
+    if nz > 3:
+        s_up[1](3)
     wait_da()
     back_out(0)
     for j in range(NH):
         back_attend(0, j)
-    for d in range(nz - 1, 0, -1):
-        s_dn[1](d)
+    for d in range(min(2, nz - 1), 0, -1):
+        s_up[1](d)
     wait_da = back_middle(1)
     r.XS[4] = chip_sum(2, 1 - x).astype(BF16)
     send(lambda: xcopy(2, 0))
     r.PF2[...] = chip_sum(2, x)
+    if nz > 3:
+        s_dn[1](3)
     wait_da()
     back_out(1)
     da_all = r.DA[...].reshape(L, D)
     r.G2[:, :, pl.ds(0, D)] = tn(r.OB[...], da_all).astype(BF16).reshape(nz, CB, D)
-    s_out[0]()
+    if nz > 3:
+        s_out[1](3)
     for j in range(NH):
         back_attend(1, j)
-    s_up[1](0)
-    s_dn[1](0)
 
     def qkv_block(bb):
         t = nn(r.HN1T[bb], r.DQ[...]).reshape(2, CB, D - LO)
@@ -809,27 +873,34 @@
         r.G1[bb, :, :, pl.ds(LO, 128)] = head.astype(BF16)
         r.G1[bb, :, :, pl.ds(384, D - 384)] = t[:, :, 128:].astype(BF16)
 
-    for k in range(nz):
-        qkv_block(2 * k + (1 - y))
-    s_qkv[0]()
+    for d in (*far, 0):
+        if d:
+            pl.when(z + d < nz)(lambda: qkv_block(2 * (z + d) + (1 - y)))
+            pl.when(z - d >= 0)(lambda: qkv_block(2 * (z - d) + (1 - y)))
+        else:
+            qkv_block(2 * z + (1 - y))
+        s_far[0](d)
+        s_own[0](d)
     for k in range(nz):
         qkv_block(2 * k + y)
-    for d in range(nz - 1, 0, -1):
-        s_out[1](d)
-
+
+    for p in range(2):
+        w = W1[:, :, :, pl.ds(LO, D - LO)].reshape(D, D - LO)
+        to_sibling(3, p, nt(r.DQ[rows_of(p)], w))
+    s_up[1](0)
     arrive(lambda: xcopy(2, 0))
     own_out = r.PF2[...] + r.XR[4].astype(F32)
     mixed_o[...] = (r.MID[x] + own_out + bias_down).astype(BF16)
-
-    for p in range(2):
-        w = W1[:, :, :, pl.ds(LO, D - LO)].reshape(D, D - LO)
-        to_sibling(3, p, nt(r.DQ[rows_of(p)], w))
     r.XS[5] = chip_sum(3, 1 - x).astype(BF16)
     send(lambda: xcopy(3, 0))
     r.PF2[...] = chip_sum(3, x)
-
-    s_qkv[1](nz - 1)
-    s_out[1](0)
+    s_out[1](2)
+    s_dn[1](2)
+    if nz > 3:
+        s_far[1](3)
+        s_own[1](3)
+    s_out[1](1)
+    s_dn[1](1)
 
     arrive(lambda: xcopy(3, 0))
     dh = r.PF2[...] + r.XR[5].astype(F32)
@@ -840,6 +911,11 @@
     gtok_o[...] = r.DMID[x] + inv * (dn - n * jnp.mean(dn * n, axis=1, keepdims=True))
     r.SGA[0:1] = jnp.sum(dh * n, axis=0, keepdims=True)
     r.SGA[2:3] = jnp.sum(r.DY[s].astype(F32), axis=0, keepdims=True)
+    s_out[1](0)
+    m_gy = lambda: copy(
+        r.G2.at[z, :, pl.ds(0, D)], r.YR2.at[z, :, pl.ds(0, D)], r.s_one.at[14 + 1], r.r_one.at[14 + 1], yp
+    )
+    send(m_gy, not_mine)
 
     def small_copy(k, slot, dev):
         return lambda: copy(r.SGA if k == 0 else r.SGS.at[k - 1], r.SGR.at[slot], r.s_sg.at[slot], r.r_sg.at[slot], dev)
@@ -849,8 +925,9 @@
         mk = small_copy(k, k, dev)
         send(mk)
         if k == 1:
-            for d in range(nz - 2, 0, -1):
-                s_qkv[1](d)
+            s_far[1](2)
+            s_own[1](2)
+            s_dn[1](0)
         arrive(mk)
         total = total + r.SGR[k]
         r.SGS[k] = total
@@ -859,15 +936,25 @@
         mk = small_copy(3, 2 + k, (2 * lax.rem(z + k, nz) + y, s))
         send(mk)
         mks.append(mk)
-    s_qkv[1](0)
+    s_far[1](1)
+    s_own[1](1)
+    s_far[1](0)
 
     m_fx = lambda: copy(r.G1.at[b, 1 - x], r.FX, r.s_one.at[11], r.r_one.at[11], xp)
     send(m_fx)
+    arrive(m_gy, mine)
+
+    def out_from_y():
+        cut = pl.ds(0, D)
+        r.G2[z, :, cut] = (r.G2[z, :, cut].astype(F32) + r.YR2[z, :, cut].astype(F32)).astype(BF16)
+
+    when(mine, out_from_y)
     done2 = r.G2[z].astype(F32)
     r.GF2[0] = done2[:RW]
     r.GF2[1] = done2[RW:]
     m_g2 = lambda: copy(r.GF2.at[1 - c], r.GR2, r.s_one.at[12], r.r_one.at[12], sib)
     send(m_g2, mine)
+    s_own[1](0)
     own = r.G1[b, x].astype(F32)
     r.GF[0, x] = own[:RW]
     r.GF[1, x] = own[RW:]
@@ -875,7 +962,6 @@
         arrive(mk)
         total = total + r.SGR[3 + k]
     sg_o[...] = total
-    not_mine = jnp.logical_not(mine)
     arrive(m_g2, not_mine)
 
     def out2_own():
@@ -905,15 +991,15 @@
     rows, D = wout.shape
     T = tokens.shape[1]
     L = ns * T
-    cols = jnp.concatenate([wup.reshape(rows, 1, 4, 2, 2, HD), wqkv.reshape(rows, 3, 4, 2, 2, HD)], axis=1)
-    w1p = jnp.transpose(cols, (3, 4, 0, 1, 2, 5)).reshape(2, 2, rows, D)
-    w1p = jnp.pad(w1p, ((0, 0), (0, 0), (0, 8), (0, 0)))
-    w2p = jnp.pad(jnp.concatenate([wout, wdown], axis=1), ((0, 8), (0, 0)))
-    smalls = jnp.stack([gattn, gffn, bup, bdown]).astype(F32)
-    smalls = jnp.pad(smalls, ((0, 4), (0, 128 - rows)))
-    scale = jnp.broadcast_to(jnp.tile(scale_param.astype(F32), 4)[None], (8, 4 * HD))
     V = pltpu.VMEM
     scratch = dict(
+        WQ=V((rows, 3 * D), BF16),
+        WU=V((rows, D), BF16),
+        WO=V((rows, D), BF16),
+        WD=V((rows, D), BF16),
+        SM=V((8, 128), F32),
+        W1P=V((2, 2, 48, D), BF16),
+        W2P=V((48, 2 * D), BF16),
         SIB1=V((2, 48, D), BF16),
         SIB2=V((48, 2 * D), BF16),
         CB1=V((HD, D), BF16),
@@ -972,19 +1058,21 @@
     )
     dma = pltpu.SemaphoreType.DMA
     scratch.update(
-        s_one=dma((14,)), r_one=dma((14,)),
-        s_up=dma((5, nz)), r_up=dma((5, nz)),
-        s_dn=dma((5, nz)), r_dn=dma((5, nz)),
-        s_y=dma((5, nz)), r_y=dma((5, nz)),
+        s_in=dma((6,)),
+        s_one=dma((16,)), r_one=dma((16,)),
+        s_up=dma((6, nz)), r_up=dma((6, nz)),
+        s_dn=dma((6, nz)), r_dn=dma((6, nz)),
+        s_y=dma((6, nz)), r_y=dma((6, nz)),
         s_e=dma((4, 2)), r_e=dma((4, 2)),
         s_x=dma((6,)), r_x=dma((6,)),
         s_h=dma((2, 2)), r_h=dma((2, 2)),
-        s_ry=dma((4, nz)), r_ry=dma((4, nz)),
-        s_ru=dma((4, nz)), r_ru=dma((4, nz)),
-        s_rd=dma((4, nz)), r_rd=dma((4, nz)),
+        s_ry=dma((5, nz)), r_ry=dma((5, nz)),
+        s_ru=dma((5, nz)), r_ru=dma((5, nz)),
+        s_rd=dma((5, nz)), r_rd=dma((5, nz)),
         s_sg=dma((2 + nz,)), r_sg=dma((2 + nz,)),
     )
     vmem = pl.BlockSpec(memory_space=pltpu.VMEM)
+    hbm = pl.BlockSpec(memory_space=pl.ANY)
     mixed, gtok, o1, o2, sg = pl.pallas_call(
         functools.partial(layer_kernel, nz, tuple(scratch)),
         out_shape=(
@@ -994,34 +1082,67 @@
             jax.ShapeDtypeStruct((rows, 2 * D), F32),
             jax.ShapeDtypeStruct((8, D), F32),
         ),
-        in_specs=[vmem] * 6,
+        in_specs=[hbm] * 6 + [vmem] * 5,
         out_specs=(vmem,) * 5,
         scratch_shapes=list(scratch.values()),
         compiler_params=pltpu.CompilerParams(
             collective_id=0, has_side_effects=True, vmem_limit_bytes=63 << 20
         ),
         name="decoder_layer",
-    )(tokens[0], cot[0], w1p, w2p, smalls, scale)
-    grads = jnp.transpose(o1.reshape(2, 2, rows, 4, 4, HD), (2, 3, 4, 1, 0, 5)).reshape(rows, 4 * D)
-    b, s = lax.axis_index("batch"), lax.axis_index("seq")
-    at = (b * ns + s) * rows
-    own = lambda v: lax.dynamic_slice(v, (at,), (rows,))
-    bias_up = jnp.transpose(sg[4:8, : 4 * HD].reshape(2, 2, 4, HD), (2, 1, 0, 3)).reshape(D)
-    scale_float = scale_param.astype(F32)
-    grad_scale = sg[3, :HD] * (soft_unit / math.sqrt(HD)) * jax.nn.sigmoid(scale_float)
-    return (
-        mixed[None],
-        gtok[None],
-        grads[:, D:],
-        o2[:, :D],
-        grads[:, :D],
-        o2[:, D:],
-        own(sg[0]),
-        own(sg[1]),
-        own(bias_up),
-        own(sg[2]),
-        grad_scale,
-    )
+    )(tokens[0], cot[0], wqkv, wout, wup, wdown, gattn, gffn, bup, bdown, scale_param)
+    mixed, gtok, gqkv, gout, gup, gdown, g_attn, g_ffn, g_bup, g_bdown, gscale = pl.pallas_call(
+        functools.partial(outputs_kernel, ns),
+        out_shape=(
+            jax.ShapeDtypeStruct((T, D), BF16),
+            jax.ShapeDtypeStruct((T, D), F32),
+            jax.ShapeDtypeStruct((rows, 3 * D), F32),
+            jax.ShapeDtypeStruct((rows, D), F32),
+            jax.ShapeDtypeStruct((rows, D), F32),
+            jax.ShapeDtypeStruct((rows, D), F32),
+            jax.ShapeDtypeStruct((rows,), F32),
+            jax.ShapeDtypeStruct((rows,), F32),
+            jax.ShapeDtypeStruct((rows,), F32),
+            jax.ShapeDtypeStruct((rows,), F32),
+            jax.ShapeDtypeStruct((HD,), F32),
+        ),
+        in_specs=[vmem] * 6,
+        out_specs=(vmem,) * 11,
+        compiler_params=pltpu.CompilerParams(vmem_limit_bytes=63 << 20),
+        name="place_outputs",
+    )(mixed, gtok, o1, o2, sg, scale_param)
+    return mixed[None], gtok[None], gqkv, gout, gup, gdown, g_attn, g_ffn, g_bup, g_bdown, gscale
+
+
+def outputs_kernel(ns, mixed, gtok, o1, o2, sg, scl, mixed_o, gtok_o, gqkv, gout, gup, gdown, *small):
+    rows, D = gup.shape
+    HW = 4 * HD
+    mixed_o[...] = mixed[...]
+    gtok_o[...] = gtok[...]
+    gout[...] = o2[:, 0:D]
+    gdown[...] = o2[:, D : 2 * D]
+    for xx in range(2):
+        for cc in range(2):
+            for t in range(4):
+                for j in range(4):
+                    v = o1[xx, cc, :, HW * t + HD * j : HW * t + HD * (j + 1)]
+                    at = HD * (4 * j + 2 * cc + xx)
+                    if t == 0:
+                        gup[:, at : at + HD] = v
+                    else:
+                        gqkv[:, D * (t - 1) + at : D * (t - 1) + at + HD] = v
+    first = (lax.axis_index("batch") * ns + lax.axis_index("seq")) * rows
+    parts = []
+    for h in range(H):
+        j, cc, xx = h // 4, (h // 2) % 2, h % 2
+        row = 4 + 2 * xx + cc
+        parts.append(sg[row : row + 1, HD * j : HD * (j + 1)])
+    bias_up = jnp.concatenate(parts, axis=1)
+    shift = lax.rem(D - first, D)
+    for ref, v in zip(small, (sg[0:1], sg[1:2], bias_up, sg[2:3])):
+        v = jnp.broadcast_to(v, (8, D))
+        ref[...] = pltpu.roll(v, shift, 1)[0, 0:rows]
+    scale = scl[...].astype(F32).reshape(1, HD)
+    small[4][...] = (sg[3:4, 0:HD] * (soft_unit / math.sqrt(HD)) / (1.0 + jnp.exp(-scale)))[0]
 
 
 def layer_step(nb, ns, *args):

time: 198 us -> 154 us (0.78)
  Pallas kernels: 173 us -> 151 us
  local copies, waits for them, and re-layouts: 18.1 us -> 0 us
  other arithmetic: 4.78 us -> 0 us
    pallas_call x1, Pallas kernels: 173 us -> 147 us  [fused_layer(): pl.pallas_call(functools.partial(layer_kernel, nz, tuple(scratch)), out_s...]
    reshape x10 -> x0, local copies, waits for them, and re-layouts: 6.58 us -> none  [the longest x1 1.85 us: fused_layer(): jnp.transpose(o1.reshape(2, 2, rows, 4, 4, HD), (2, 3, 4, 1, 0, 5))]
    slice x5 -> x0, local copies, waits for them, and re-layouts: 4.97 us -> none  [the longest x1 1.8 us: fused_layer(): o2[:, D:]]
    pallas_call x0 -> x1, Pallas kernels: none -> 3.51 us  [fused_layer(): pl.pallas_call(functools.partial(outputs_kernel, ns), out_shape=(jax.Shap...]
where the time goes in v2:
time: 154 us; the launch traced here: 151 us
  Pallas kernels  151 us (98%)
    pallas_call x1, Pallas kernels, fused_layer(): pl.pallas_call(functools.partial(layer_kernel, nz, tuple(scratch)), out_s...  147 us
    pallas_call x1, Pallas kernels, fused_layer(): pl.pallas_call(functools.partial(outputs_kernel, ns), out_shape=(jax.Shap...  3.51 us

profile of v2, /device:TPU:0, one launch (start us, length us, event | category | flops | bytes accessed | tf_op | source)
XLA Modules:
  0.0 151.5 jit_solution(6428272802164754837)
XLA Ops:
  0.6 147.1 %decoder_layer.1 = (bf16[128,1280]{1,0:T(8,128)(2,1)}, f32[128,1280]{1,0:T(8,128)}, f32[2,2,40,1280]{3,2,1,0:T(8,128)}, f32[40,2560]{1,0:T(8,128)}, f32[8,1280]{1,0:T(8,128)}) custom-call(bf16[128,1280]{1,0:T(8,128)(2,1)} %bitcast.4, bf16[128,1280]{1,0:T(8,128)(2,1)} %bitcast.5, bf16[40,3840]{1,0:T(8,128)(2,1)} %wqkv.1, bf16[40,1280]{1,0:T(8,128)(2,1)} %wout.1, ...), custom_call_target="tpu_custom_call" | custom-call | tf_op jit(solution)/shard_map/decoder_layer/pallas_call | solution.py:1076
  147.8 3.5 %place_outputs.1 = (bf16[128,1280]{1,0:T(8,128)(2,1)}, f32[128,1280]{1,0:T(8,128)}, f32[40,3840]{1,0:T(8,128)}, f32[40,1280]{1,0:T(8,128)}, f32[40,1280]{1,0:T(8...) custom-call(bf16[128,1280]{1,0:T(8,128)(2,1)} %get-tuple-element.27., ...), custom_call_target="tpu_custom_call" | custom-call | tf_op jit(solution)/shard_map/place_outputs/pallas_call | solution.py:1093

commit v3 on v2

--- a/solution.py
+++ b/solution.py
@@ -388,8 +388,8 @@
     m_sib1 = lambda: copy(r.W1P.at[1 - c], r.SIB1, r.s_one.at[0], r.r_one.at[0], sib)
     m_ssib = lambda: copy(r.SM, r.S.at[b, s], r.s_one.at[1], r.r_one.at[1], sib)
     m_sib2 = lambda: copy(r.W2P, r.SIB2, r.s_one.at[2], r.r_one.at[2], sib)
+    send(m_ssib)
     send(m_sib1)
-    send(m_ssib)
     fetches[2].wait()
     fetches[3].wait()
     r.W2P[0:RW, 0:D] = r.WO[...]
@@ -403,11 +403,24 @@
         hi = jnp.where(c == 0, other, own)
         return jnp.concatenate([lo, hi], axis=0).astype(BF16)
 
+    m_ssib_r = lambda: copy(r.SM, r.S.at[b, 2 * x + (1 - c)], r.s_one.at[1], r.r_one.at[1], sib)
+    arrive(m_ssib_r)
+    m_xs = lambda: copy(
+        r.S.at[b, pl.ds(2 * x, 2)], r.S.at[b, pl.ds(2 * x, 2)], r.s_one.at[4], r.r_one.at[4], xp
+    )
+    send(m_xs)
     arrive(m_sib1)
     r.CB1[...] = chip_rows(r.W1P[c, 1 - x], r.SIB1[1 - x])
-    m_x1 = lambda: copy(r.CB1, r.W1.at[b, x], r.s_one.at[3], r.r_one.at[3], xp)
-    send(m_x1)
+    half = (D - LO) // 2
+    cuts = (pl.ds(LO, half), pl.ds(LO + half, half), pl.ds(0, LO))
+
+    def m_x1(k, xx):
+        return copy(r.CB1.at[:, cuts[k]], r.W1.at[b, xx, :, cuts[k]], r.s_x1.at[k], r.r_x1.at[k], xp)
+
+    for k in range(3):
+        send(lambda k=k: m_x1(k, x))
     r.W1[b, x] = chip_rows(r.W1P[c, x], r.SIB1[x])
+
     def gather_item(idx, block, zcond, passes_y=True):
         up = lambda zz: copy(block(zz, y), block(zz, y), r.s_up.at[idx, zz], r.r_up.at[idx, zz], zup)
         dn = lambda zz: copy(block(zz, y), block(zz, y), r.s_dn.at[idx, zz], r.r_dn.at[idx, zz], zdn)
@@ -445,19 +458,25 @@
     mine = c == y
     not_mine = c != y
     g_s = gather_item(0, lambda zz, q: r.S.at[2 * zz + q], None)
-    g_own = gather_item(1, lambda zz, q: r.W1.at[2 * zz + q, x, :, pl.ds(LO, D - LO)], None)
-    g_oth = gather_item(2, lambda zz, q: r.W1.at[2 * zz + q, 1 - x, :, pl.ds(LO, D - LO)], None)
-    g_out = gather_item(3, lambda zz, q: r.W2.at[zz, :, pl.ds(0, D)], None, False)
-    g_up = gather_item(4, lambda zz, q: r.W1.at[2 * zz + q, :, :, pl.ds(0, LO)], None)
-    g_dn = gather_item(5, lambda zz, q: r.W2.at[zz, :, pl.ds(D, D)], mine)
-
-    g_own[0]()
-    m_ssib_r = lambda: copy(r.SM, r.S.at[b, 2 * x + (1 - c)], r.s_one.at[1], r.r_one.at[1], sib)
-    arrive(m_ssib_r)
-    m_xs = lambda: copy(
-        r.S.at[b, pl.ds(2 * x, 2)], r.S.at[b, pl.ds(2 * x, 2)], r.s_one.at[4], r.r_one.at[4], xp
-    )
-    send(m_xs)
+    g_own = [gather_item(1 + k, lambda zz, q, k=k: r.W1.at[2 * zz + q, x, :, cuts[k]], None) for k in range(2)]
+    g_oth = [
+        gather_item(3 + k, lambda zz, q, k=k: r.W1.at[2 * zz + q, 1 - x, :, cuts[k]], None) for k in range(2)
+    ]
+    g_out = gather_item(5, lambda zz, q: r.W2.at[zz, :, pl.ds(0, D)], None, False)
+    g_up = gather_item(6, lambda zz, q: r.W1.at[2 * zz + q, :, :, pl.ds(0, LO)], None)
+    g_dn = gather_item(7, lambda zz, q: r.W2.at[zz, :, pl.ds(D, D)], mine)
+
+    g_own[0][0]()
+    g_own[1][0]()
+    m_xs_r = lambda: copy(
+        r.S.at[b, pl.ds(2 - 2 * x, 2)],
+        r.S.at[b, pl.ds(2 - 2 * x, 2)],
+        r.s_one.at[4],
+        r.r_one.at[4],
+        xp,
+    )
+    arrive(m_xs_r)
+    g_s[0]()
     fetches[4].wait()
     fetches[5].wait()
     own_tok, own_cot = r.X.at[s], r.DY.at[s]
@@ -478,47 +497,43 @@
     m_y2 = lambda: copy(
         r.W2.at[z, :, pl.ds(0, D)], r.W2.at[z, :, pl.ds(0, D)], r.s_one.at[14], r.r_one.at[14], yp
     )
-
-    m_x1_r = lambda: copy(r.CB1, r.W1.at[b, 1 - x], r.s_one.at[3], r.r_one.at[3], xp)
-    m_xs_r = lambda: copy(
-        r.S.at[b, pl.ds(2 - 2 * x, 2)],
-        r.S.at[b, pl.ds(2 - 2 * x, 2)],
-        r.s_one.at[4],
-        r.r_one.at[4],
-        xp,
-    )
     sx = 2 * (1 - x) + c
     so = 2 * (1 - x) + (1 - c)
     ss = 2 * x + (1 - c)
     fwd = lambda name, k, src_i: copy(
         name.at[src_i], name.at[src_i], r.s_one.at[k], r.r_one.at[k], sib
     )
-    arrive(m_x1_r)
-    g_oth[0]()
-    arrive(m_xs_r)
-    g_s[0]()
+    arrive(lambda: m_x1(0, 1 - x))
+    g_oth[0][0]()
+    g_own[0][1](1)
+    arrive(lambda: m_x1(1, 1 - x))
+    g_oth[1][0]()
     send(m_y2, mine)
-    g_own[1](1)
+    g_own[1][1](1)
+    g_s[1](1)
+    arrive(lambda: m_x1(2, 1 - x))
+    g_oth[0][1](1)
+    g_oth[1][1](1)
+    g_own[0][1](2)
+    g_own[1][1](2)
+    g_s[1](2)
     arrive(lambda: copy(own_tok, r.X.at[sx], r.s_one.at[5], r.r_one.at[5], xp))
     send(lambda: fwd(r.X, 9, sx))
-    g_oth[1](1)
-    g_s[1](1)
+    g_oth[0][1](2)
     arrive(m_y2, not_mine)
     g_out[0]()
-    g_own[1](2)
+    g_oth[1][1](2)
+    for d in range(3, nz):
+        g_own[0][1](d)
+        g_own[1][1](d)
+        g_s[1](d)
+        g_oth[0][1](d)
+        g_oth[1][1](d)
     arrive(lambda: copy(own_tok, r.X.at[ss], r.s_one.at[6], r.r_one.at[6], sib))
     arrive(lambda: fwd(r.X, 9, so))
-    g_oth[1](2)
-    g_s[1](2)
     arrive(lambda: copy(own_cot, r.DY.at[sx], r.s_one.at[7], r.r_one.at[7], xp))
     send(lambda: fwd(r.DY, 10, sx))
     arrive(lambda: copy(own_cot, r.DY.at[ss], r.s_one.at[8], r.r_one.at[8], sib))
-    for d in range(3, nz):
-        g_own[1](d)
-        g_oth[1](d)
-        g_s[1](d)
-    g_up[0]()
-    g_dn[0]()
     g_out[1](1)
     g_s[2]()
     arrive(lambda: fwd(r.DY, 10, so))
@@ -556,10 +571,10 @@
         r.HN1[pl.ds(k * T, T)] = hn.astype(BF16)
         r.HN1T[:, :, pl.ds(k * T, T)] = hn.T.astype(BF16).reshape(2 * nz, 2 * CB, T)
     g_out[1](2)
-    g_own[2]()
-    g_oth[2]()
-    for d in range(3, nz):
-        g_out[1](d)
+    g_up[0]()
+    g_dn[0]()
+    for g in (*g_own, *g_oth):
+        g[2]()
 
     W1 = r.W1
     W2 = r.W2
@@ -642,19 +657,21 @@
 
     for j in range(NH):
         attend(0, j)
+    for d in range(3, nz):
+        g_out[1](d)
     out_proj(0)
-    g_up[1](1)
     attend(1, 0)
     attend(1, 1)
     to_x(0, 0)
+    g_up[1](1)
     g_dn[1](1)
     attend(1, 2)
     attend(1, 3)
     out_proj(1)
+    to_x(0, 1)
     for d in range(2, nz):
         g_up[1](d)
         g_dn[1](d)
-    to_x(0, 1)
 
     r.SGA[...] = jnp.zeros_like(r.SGA)
 
@@ -699,7 +716,6 @@
     wait_hn()
     feed(1)
     transpose_hn2(1)
-    to_x(1, 1)
 
     def scatter_item(idx, part, yr, zu, zd, zcond, y_first=True):
         yc = lambda zz: copy(part(zz, 1 - y), yr(zz), r.s_ry.at[idx, zz], r.r_ry.at[idx, zz], yp)
@@ -769,8 +785,8 @@
             None,
         )
 
-    def w2_item(idx, lo, zcond, y_first):
-        cut = pl.ds(lo, D)
+    def w2_item(idx, lo, width, zcond, y_first):
+        cut = pl.ds(lo, width)
         return scatter_item(
             idx,
             lambda zz, q: r.G2.at[zz, :, cut],
@@ -781,8 +797,9 @@
             y_first,
         )
 
-    s_dn = w2_item(1, D, mine, True)
-    s_out = w2_item(2, 0, None, False)
+    s_dn = w2_item(1, D, D, mine, True)
+    s_out = w2_item(2, 0, D // 2, None, False)
+    s_out2 = w2_item(5, D // 2, D // 2, mine, True)
     s_far = qkv_item(3, 1 - x)
     s_own = qkv_item(4, x)
 
@@ -790,6 +807,7 @@
     r.G1[:, :, :, 0:384] = gu.astype(BF16).reshape(2 * nz, 2, CB, 384)
     for d in (*far, 0):
         s_up[0](d)
+    to_x(1, 1)
     dy_all = r.DY[...].reshape(L, D)
     r.G2[:, :, pl.ds(D, D)] = tn(r.ACT[...], dy_all).astype(BF16).reshape(nz, CB, D)
     for d in (*far, 0):
@@ -850,12 +868,13 @@
     back_out(0)
     for j in range(NH):
         back_attend(0, j)
-    for d in range(min(2, nz - 1), 0, -1):
-        s_up[1](d)
+    if nz > 2:
+        s_up[1](2)
     wait_da = back_middle(1)
     r.XS[4] = chip_sum(2, 1 - x).astype(BF16)
     send(lambda: xcopy(2, 0))
     r.PF2[...] = chip_sum(2, x)
+    s_up[1](1)
     if nz > 3:
         s_dn[1](3)
     wait_da()
@@ -864,6 +883,8 @@
     r.G2[:, :, pl.ds(0, D)] = tn(r.OB[...], da_all).astype(BF16).reshape(nz, CB, D)
     if nz > 3:
         s_out[1](3)
+    for d in (*far, 0):
+        s_out2[0](d)
     for j in range(NH):
         back_attend(1, j)
 
@@ -873,14 +894,13 @@
         r.G1[bb, :, :, pl.ds(LO, 128)] = head.astype(BF16)
         r.G1[bb, :, :, pl.ds(384, D - 384)] = t[:, :, 128:].astype(BF16)
 
-    for d in (*far, 0):
-        if d:
-            pl.when(z + d < nz)(lambda: qkv_block(2 * (z + d) + (1 - y)))
-            pl.when(z - d >= 0)(lambda: qkv_block(2 * (z - d) + (1 - y)))
-        else:
-            qkv_block(2 * z + (1 - y))
+    for d in far:
+        pl.when(z + d < nz)(lambda: qkv_block(2 * (z + d) + (1 - y)))
+        pl.when(z - d >= 0)(lambda: qkv_block(2 * (z - d) + (1 - y)))
         s_far[0](d)
-        s_own[0](d)
+        if d > 1:
+            s_own[0](d)
+    qkv_block(2 * z + (1 - y))
     for k in range(nz):
         qkv_block(2 * k + y)
 
@@ -888,19 +908,25 @@
         w = W1[:, :, :, pl.ds(LO, D - LO)].reshape(D, D - LO)
         to_sibling(3, p, nt(r.DQ[rows_of(p)], w))
     s_up[1](0)
+    if nz > 2:
+        s_dn[1](2)
     arrive(lambda: xcopy(2, 0))
     own_out = r.PF2[...] + r.XR[4].astype(F32)
     mixed_o[...] = (r.MID[x] + own_out + bias_down).astype(BF16)
     r.XS[5] = chip_sum(3, 1 - x).astype(BF16)
     send(lambda: xcopy(3, 0))
     r.PF2[...] = chip_sum(3, x)
-    s_out[1](2)
-    s_dn[1](2)
+    s_dn[1](1)
+    if nz > 2:
+        s_out[1](2)
     if nz > 3:
+        s_out2[1](3)
         s_far[1](3)
         s_own[1](3)
     s_out[1](1)
-    s_dn[1](1)
+    if nz > 2:
+        s_out2[1](2)
+    s_dn[1](0)
 
     arrive(lambda: xcopy(3, 0))
     dh = r.PF2[...] + r.XR[5].astype(F32)
@@ -911,23 +937,32 @@
     gtok_o[...] = r.DMID[x] + inv * (dn - n * jnp.mean(dn * n, axis=1, keepdims=True))
     r.SGA[0:1] = jnp.sum(dh * n, axis=0, keepdims=True)
     r.SGA[2:3] = jnp.sum(r.DY[s].astype(F32), axis=0, keepdims=True)
-    s_out[1](0)
-    m_gy = lambda: copy(
-        r.G2.at[z, :, pl.ds(0, D)], r.YR2.at[z, :, pl.ds(0, D)], r.s_one.at[14 + 1], r.r_one.at[14 + 1], yp
-    )
-    send(m_gy, not_mine)
 
     def small_copy(k, slot, dev):
-        return lambda: copy(r.SGA if k == 0 else r.SGS.at[k - 1], r.SGR.at[slot], r.s_sg.at[slot], r.r_sg.at[slot], dev)
+        return lambda: copy(
+            r.SGA if k == 0 else r.SGS.at[k - 1], r.SGR.at[slot], r.s_sg.at[slot], r.r_sg.at[slot], dev
+        )
 
     total = r.SGA[...]
     for k, dev in enumerate((sib, xp, yp)):
         mk = small_copy(k, k, dev)
         send(mk)
-        if k == 1:
+        if k == 0 and nz > 2:
             s_far[1](2)
-            s_own[1](2)
-            s_dn[1](0)
+        if k == 2:
+            cut_o = pl.ds(0, D // 2)
+            s_out[1](0)
+            m_gy = lambda: copy(
+                r.G2.at[z, :, cut_o], r.YR2.at[z, :, cut_o], r.s_one.at[15], r.r_one.at[15], yp
+            )
+            send(m_gy, not_mine)
+            s_far[0](0)
+            s_own[0](1)
+            s_own[0](0)
+            if nz > 2:
+                s_own[1](2)
+            s_far[1](1)
+            s_out2[1](1)
         arrive(mk)
         total = total + r.SGR[k]
         r.SGS[k] = total
@@ -936,17 +971,11 @@
         mk = small_copy(3, 2 + k, (2 * lax.rem(z + k, nz) + y, s))
         send(mk)
         mks.append(mk)
-    s_far[1](1)
-    s_own[1](1)
-    s_far[1](0)
-
-    m_fx = lambda: copy(r.G1.at[b, 1 - x], r.FX, r.s_one.at[11], r.r_one.at[11], xp)
-    send(m_fx)
+    s_out2[1](0)
     arrive(m_gy, mine)
 
     def out_from_y():
-        cut = pl.ds(0, D)
-        r.G2[z, :, cut] = (r.G2[z, :, cut].astype(F32) + r.YR2[z, :, cut].astype(F32)).astype(BF16)
+        r.G2[z, :, cut_o] = (r.G2[z, :, cut_o].astype(F32) + r.YR2[z, :, cut_o].astype(F32)).astype(BF16)
 
     when(mine, out_from_y)
     done2 = r.G2[z].astype(F32)
@@ -954,10 +983,9 @@
     r.GF2[1] = done2[RW:]
     m_g2 = lambda: copy(r.GF2.at[1 - c], r.GR2, r.s_one.at[12], r.r_one.at[12], sib)
     send(m_g2, mine)
-    s_own[1](0)
-    own = r.G1[b, x].astype(F32)
-    r.GF[0, x] = own[:RW]
-    r.GF[1, x] = own[RW:]
+    s_far[1](0)
+    m_fx = lambda: copy(r.G1.at[b, 1 - x], r.FX, r.s_one.at[11], r.r_one.at[11], xp)
+    send(m_fx)
     for k, mk in enumerate(mks):
         arrive(mk)
         total = total + r.SGR[3 + k]
@@ -972,15 +1000,28 @@
 
     when(mine, out2_own)
     when(not_mine, out2_sib)
+
+    def hand_over(k, xx, block):
+        done = block.astype(F32)
+        r.GF[0, xx] = done[:RW]
+        r.GF[1, xx] = done[RW:]
+        mk = lambda i: copy(r.GF.at[1 - c, i], r.GRV.at[i], r.s_gf.at[k], r.r_gf.at[k], sib)
+        send(lambda: mk(xx))
+        o1[xx, c] = r.GF[c, xx]
+
+        def take():
+            arrive(lambda: mk(xx))
+            o1[xx, 1 - c] = r.GRV[xx]
+
+        return take
+
+    s_own[1](1)
     arrive(m_fx)
-    other = r.FX[...].astype(F32)
-    r.GF[0, 1 - x] = other[:RW]
-    r.GF[1, 1 - x] = other[RW:]
-    m_gf = lambda: copy(r.GF.at[1 - c], r.GRV, r.s_one.at[13], r.r_one.at[13], sib)
-    send(m_gf)
-    o1[:, c] = r.GF[c]
-    arrive(m_gf)
-    o1[:, 1 - c] = r.GRV[...]
+    take_other = hand_over(0, 1 - x, r.FX[...])
+    s_own[1](0)
+    take_own = hand_over(1, x, r.G1[b, x])
+    take_other()
+    take_own()
 
     for make, cond in drains:
         when(cond, lambda make=make: make().wait_send())
@@ -1059,16 +1100,18 @@
     dma = pltpu.SemaphoreType.DMA
     scratch.update(
         s_in=dma((6,)),
+        s_x1=dma((3,)), r_x1=dma((3,)),
+        s_gf=dma((2,)), r_gf=dma((2,)),
         s_one=dma((16,)), r_one=dma((16,)),
-        s_up=dma((6, nz)), r_up=dma((6, nz)),
-        s_dn=dma((6, nz)), r_dn=dma((6, nz)),
-        s_y=dma((6, nz)), r_y=dma((6, nz)),
+        s_up=dma((8, nz)), r_up=dma((8, nz)),
+        s_dn=dma((8, nz)), r_dn=dma((8, nz)),
+        s_y=dma((8, nz)), r_y=dma((8, nz)),
         s_e=dma((4, 2)), r_e=dma((4, 2)),
         s_x=dma((6,)), r_x=dma((6,)),
         s_h=dma((2, 2)), r_h=dma((2, 2)),
-        s_ry=dma((5, nz)), r_ry=dma((5, nz)),
-        s_ru=dma((5, nz)), r_ru=dma((5, nz)),
-        s_rd=dma((5, nz)), r_rd=dma((5, nz)),
+        s_ry=dma((6, nz)), r_ry=dma((6, nz)),
+        s_ru=dma((6, nz)), r_ru=dma((6, nz)),
+        s_rd=dma((6, nz)), r_rd=dma((6, nz)),
         s_sg=dma((2 + nz,)), r_sg=dma((2 + nz,)),
     )
     vmem = pl.BlockSpec(memory_space=pltpu.VMEM)

time: 154 us -> 141 us (0.916); the launches traced: 151 us -> 141 us
  Pallas kernels: 151 us -> 140 us
    pallas_call x1, Pallas kernels: 147 us -> 137 us  [fused_layer(): pl.pallas_call(functools.partial(layer_kernel, nz, tuple(scratch)), out_s...]
where the time goes in v3:
time: 141 us
  Pallas kernels  140 us (99%)
    pallas_call x1, Pallas kernels, fused_layer(): pl.pallas_call(functools.partial(layer_kernel, nz, tuple(scratch)), out_s...  137 us
    pallas_call x1, Pallas kernels, fused_layer(): pl.pallas_call(functools.partial(outputs_kernel, ns), out_shape=(jax.Shap...  3.51 us

profile of v3, /device:TPU:0, one launch (start us, length us, event | category | flops | bytes accessed | tf_op | source)
XLA Modules:
  0.0 141.2 jit_solution(4493991519833113707)
XLA Ops:
  0.6 136.8 %decoder_layer.1 = (bf16[128,1280]{1,0:T(8,128)(2,1)}, f32[128,1280]{1,0:T(8,128)}, f32[2,2,40,1280]{3,2,1,0:T(8,128)}, f32[40,2560]{1,0:T(8,128)}, f32[8,1280]{1,0:T(8,128)}) custom-call(bf16[128,1280]{1,0:T(8,128)(2,1)} %bitcast.4, bf16[128,1280]{1,0:T(8,128)(2,1)} %bitcast.5, bf16[40,3840]{1,0:T(8,128)(2,1)} %wqkv.1, bf16[40,1280]{1,0:T(8,128)(2,1)} %wout.1, ...), custom_call_target="tpu_custom_call" | custom-call | tf_op jit(solution)/shard_map/decoder_layer/pallas_call | solution.py:1119
  137.5 3.5 %place_outputs.1 = (bf16[128,1280]{1,0:T(8,128)(2,1)}, f32[128,1280]{1,0:T(8,128)}, f32[40,3840]{1,0:T(8,128)}, f32[40,1280]{1,0:T(8,128)}, f32[40,1280]{1,0:T(8...) custom-call(bf16[128,1280]{1,0:T(8,128)(2,1)} %get-tuple-element.27., ...), custom_call_target="tpu_custom_call" | custom-call | tf_op jit(solution)/shard_map/place_outputs/pallas_call | solution.py:1136

commit v4 on v3

--- a/solution.py
+++ b/solution.py
@@ -765,7 +765,7 @@
         return start, step
 
     far = range(nz - 1, 0, -1)
-    cut_up, cut_qkv = pl.ds(0, LO), pl.ds(LO, D - LO)
+    cut_up = pl.ds(0, LO)
     s_up = scatter_item(
         0,
         lambda zz, q: r.G1.at[2 * zz + q, :, :, cut_up],
@@ -775,15 +775,26 @@
         None,
     )
 
-    def qkv_item(idx, xx):
+    def qkv_item(idx, xx, cut):
         return scatter_item(
             idx,
-            lambda zz, q: r.G1.at[2 * zz + q, xx, :, cut_qkv],
-            lambda zz: r.YR1.at[zz, xx, :, cut_qkv],
-            lambda zz: r.ZU1.at[zz - 1, xx, :, cut_qkv],
-            lambda zz: r.ZD1.at[zz, xx, :, cut_qkv],
+            lambda zz, q: r.G1.at[2 * zz + q, xx, :, cut],
+            lambda zz: r.YR1.at[zz, xx, :, cut],
+            lambda zz: r.ZU1.at[zz - 1, xx, :, cut],
+            lambda zz: r.ZD1.at[zz, xx, :, cut],
             None,
         )
+
+    def together(items):
+        def start(d):
+            for it in items:
+                it[0](d)
+
+        def step(d):
+            for it in items:
+                it[1](d)
+
+        return start, step
 
     def w2_item(idx, lo, width, zcond, y_first):
         cut = pl.ds(lo, width)
@@ -798,10 +809,12 @@
         )
 
     s_dn = w2_item(1, D, D, mine, True)
-    s_out = w2_item(2, 0, D // 2, None, False)
-    s_out2 = w2_item(5, D // 2, D // 2, mine, True)
-    s_far = qkv_item(3, 1 - x)
-    s_own = qkv_item(4, x)
+    WZ = D // 2
+    s_out = w2_item(2, 0, WZ, None, False)
+    s_out2 = w2_item(5, WZ, D - WZ, mine, True) if WZ < D else ((lambda d: None), (lambda d: None))
+    fars = [qkv_item(3, 1 - x, cuts[0]), qkv_item(6, 1 - x, cuts[1])]
+    owns = [qkv_item(4, x, cuts[0]), qkv_item(7, x, cuts[1])]
+    s_far, s_own = together(fars), together(owns)
 
     gu = nn(r.HN2T[...].reshape(D, L), r.DUP[...])
     r.G1[:, :, :, 0:384] = gu.astype(BF16).reshape(2 * nz, 2, CB, 384)
@@ -898,9 +911,10 @@
         pl.when(z + d < nz)(lambda: qkv_block(2 * (z + d) + (1 - y)))
         pl.when(z - d >= 0)(lambda: qkv_block(2 * (z - d) + (1 - y)))
         s_far[0](d)
-        if d > 1:
-            s_own[0](d)
+        s_own[0](d)
     qkv_block(2 * z + (1 - y))
+    s_far[0](0)
+    s_own[0](0)
     for k in range(nz):
         qkv_block(2 * k + y)
 
@@ -923,10 +937,13 @@
         s_out2[1](3)
         s_far[1](3)
         s_own[1](3)
+    s_dn[1](0)
+    if nz > 2:
+        s_far[1](2)
     s_out[1](1)
     if nz > 2:
         s_out2[1](2)
-    s_dn[1](0)
+        s_own[1](2)
 
     arrive(lambda: xcopy(3, 0))
     dh = r.PF2[...] + r.XR[5].astype(F32)
@@ -947,21 +964,25 @@
     for k, dev in enumerate((sib, xp, yp)):
         mk = small_copy(k, k, dev)
         send(mk)
-        if k == 0 and nz > 2:
-            s_far[1](2)
         if k == 2:
-            cut_o = pl.ds(0, D // 2)
+            s_far[1](1)
+            s_own[1](1)
+            cut_o = pl.ds(0, WZ)
             s_out[1](0)
             m_gy = lambda: copy(
                 r.G2.at[z, :, cut_o], r.YR2.at[z, :, cut_o], r.s_one.at[15], r.r_one.at[15], yp
             )
             send(m_gy, not_mine)
-            s_far[0](0)
-            s_own[0](1)
-            s_own[0](0)
-            if nz > 2:
-                s_own[1](2)
-            s_far[1](1)
+            ends = (pl.ds(0, LO + half), pl.ds(LO + half, half))
+
+            def m_fx(k):
+                return copy(
+                    r.G1.at[b, 1 - x, :, ends[k]], r.FX.at[:, ends[k]], r.s_fx.at[k], r.r_fx.at[k], xp
+                )
+
+            for h in range(2):
+                fars[h][1](0)
+                send(lambda h=h: m_fx(h))
             s_out2[1](1)
         arrive(mk)
         total = total + r.SGR[k]
@@ -972,6 +993,31 @@
         send(mk)
         mks.append(mk)
     s_out2[1](0)
+
+    def hand_over(k, h, xx, block):
+        cut = ends[h]
+        done = block.astype(F32)
+        r.GF[0, xx, :, cut] = done[:RW]
+        r.GF[1, xx, :, cut] = done[RW:]
+        mk = lambda: copy(
+            r.GF.at[1 - c, xx, :, cut], r.GRV.at[xx, :, cut], r.s_gf.at[k, h], r.r_gf.at[k, h], sib
+        )
+        send(mk)
+        o1[xx, c, :, cut] = r.GF[c, xx, :, cut]
+
+        def take():
+            arrive(mk)
+            o1[xx, 1 - c, :, cut] = r.GRV[xx, :, cut]
+
+        return take
+
+    takes = []
+    for h in range(2):
+        arrive(lambda h=h: m_fx(h))
+        takes.append(hand_over(0, h, 1 - x, r.FX[:, ends[h]]))
+    for h in range(2):
+        owns[h][1](0)
+        takes.append(hand_over(1, h, x, r.G1[b, x, :, ends[h]]))
     arrive(m_gy, mine)
 
     def out_from_y():
@@ -983,9 +1029,8 @@
     r.GF2[1] = done2[RW:]
     m_g2 = lambda: copy(r.GF2.at[1 - c], r.GR2, r.s_one.at[12], r.r_one.at[12], sib)
     send(m_g2, mine)
-    s_far[1](0)
-    m_fx = lambda: copy(r.G1.at[b, 1 - x], r.FX, r.s_one.at[11], r.r_one.at[11], xp)
-    send(m_fx)
+    for take in takes:
+        take()
     for k, mk in enumerate(mks):
         arrive(mk)
         total = total + r.SGR[3 + k]
@@ -1000,28 +1045,6 @@
 
     when(mine, out2_own)
     when(not_mine, out2_sib)
-
-    def hand_over(k, xx, block):
-        done = block.astype(F32)
-        r.GF[0, xx] = done[:RW]
-        r.GF[1, xx] = done[RW:]
-        mk = lambda i: copy(r.GF.at[1 - c, i], r.GRV.at[i], r.s_gf.at[k], r.r_gf.at[k], sib)
-        send(lambda: mk(xx))
-        o1[xx, c] = r.GF[c, xx]
-
-        def take():
-            arrive(lambda: mk(xx))
-            o1[xx, 1 - c] = r.GRV[xx]
-
-        return take
-
-    s_own[1](1)
-    arrive(m_fx)
-    take_other = hand_over(0, 1 - x, r.FX[...])
-    s_own[1](0)
-    take_own = hand_over(1, x, r.G1[b, x])
-    take_other()
-    take_own()
 
     for make, cond in drains:
         when(cond, lambda make=make: make().wait_send())
@@ -1101,17 +1124,18 @@
     scratch.update(
         s_in=dma((6,)),
         s_x1=dma((3,)), r_x1=dma((3,)),
-        s_gf=dma((2,)), r_gf=dma((2,)),
+        s_gf=dma((2, 2)), r_gf=dma((2, 2)),
+        s_fx=dma((2,)), r_fx=dma((2,)),
         s_one=dma((16,)), r_one=dma((16,)),
-        s_up=dma((8, nz)), r_up=dma((8, nz)),
-        s_dn=dma((8, nz)), r_dn=dma((8, nz)),
-        s_y=dma((8, nz)), r_y=dma((8, nz)),
+        s_up=dma((9, nz)), r_up=dma((9, nz)),
+        s_dn=dma((9, nz)), r_dn=dma((9, nz)),
+        s_y=dma((9, nz)), r_y=dma((9, nz)),
         s_e=dma((4, 2)), r_e=dma((4, 2)),
         s_x=dma((6,)), r_x=dma((6,)),
         s_h=dma((2, 2)), r_h=dma((2, 2)),
-        s_ry=dma((6, nz)), r_ry=dma((6, nz)),
-        s_ru=dma((6, nz)), r_ru=dma((6, nz)),
-        s_rd=dma((6, nz)), r_rd=dma((6, nz)),
+        s_ry=dma((8, nz)), r_ry=dma((8, nz)),
+        s_ru=dma((8, nz)), r_ru=dma((8, nz)),
+        s_rd=dma((8, nz)), r_rd=dma((8, nz)),
         s_sg=dma((2 + nz,)), r_sg=dma((2 + nz,)),
     )
     vmem = pl.BlockSpec(memory_space=pltpu.VMEM)

time: 141 us -> 140 us (level)
  Pallas kernels: 140 us -> 138 us
    pallas_call x1, Pallas kernels: 137 us -> 135 us  [fused_layer(): pl.pallas_call(functools.partial(layer_kernel, nz, tuple(scratch)), out_s...]
where the time goes in v4:
time: 140 us; the launch traced here: 139 us
  Pallas kernels  138 us (99%)
    pallas_call x1, Pallas kernels, fused_layer(): pl.pallas_call(functools.partial(layer_kernel, nz, tuple(scratch)), out_s...  135 us
    pallas_call x1, Pallas kernels, fused_layer(): pl.pallas_call(functools.partial(outputs_kernel, ns), out_shape=(jax.Shap...  3.51 us

profile of v4, /device:TPU:0, one launch (start us, length us, event | category | flops | bytes accessed | tf_op | source)
XLA Modules:
  0.0 139.2 jit_solution(13425172584597972102)
XLA Ops:
  0.6 134.8 %decoder_layer.1 = (bf16[128,1280]{1,0:T(8,128)(2,1)}, f32[128,1280]{1,0:T(8,128)}, f32[2,2,40,1280]{3,2,1,0:T(8,128)}, f32[40,2560]{1,0:T(8,128)}, f32[8,1280]{1,0:T(8,128)}) custom-call(bf16[128,1280]{1,0:T(8,128)(2,1)} %bitcast.4, bf16[128,1280]{1,0:T(8,128)(2,1)} %bitcast.5, bf16[40,3840]{1,0:T(8,128)(2,1)} %wqkv.1, bf16[40,1280]{1,0:T(8,128)(2,1)} %wout.1, ...), custom_call_target="tpu_custom_call" | custom-call | tf_op jit(solution)/shard_map/decoder_layer/pallas_call | solution.py:1143
  135.5 3.5 %place_outputs.1 = (bf16[128,1280]{1,0:T(8,128)(2,1)}, f32[128,1280]{1,0:T(8,128)}, f32[40,3840]{1,0:T(8,128)}, f32[40,1280]{1,0:T(8,128)}, f32[40,1280]{1,0:T(8...) custom-call(bf16[128,1280]{1,0:T(8,128)(2,1)} %get-tuple-element.27., ...), custom_call_target="tpu_custom_call" | custom-call | tf_op jit(solution)/shard_map/place_outputs/pallas_call | solution.py:1160

commit v5 on v4

--- a/solution.py
+++ b/solution.py
@@ -361,13 +361,20 @@
                 (wdown, r.WD),
                 (tok, r.X.at[s]),
                 (cot, r.DY.at[s]),
+                (ga, r.V0),
+                (gf, r.V1),
+                (bu, r.V2),
+                (bd, r.V3),
+                (scl, r.V4),
             )
         )
     ]
     for f in fetches:
         f.start()
-    small_rows = [v[...].astype(F32).reshape(1, RW) for v in (ga, gf, bu, bd)]
     r.SM[...] = jnp.zeros_like(r.SM)
+    for k in range(6, 11):
+        fetches[k].wait()
+    small_rows = [v[...].astype(F32).reshape(1, RW) for v in (r.V0, r.V1, r.V2, r.V3)]
     for k, row in enumerate(small_rows):
         r.SM[k : k + 1, 0:RW] = row
     fetches[0].wait()
@@ -559,7 +566,7 @@
     gain_ffn = r.ROWS[1:2]
     bias_down = r.ROWS[3:4]
     bias_up = r.BUP[2:3]
-    scale = scl[...].astype(F32).reshape(1, HD)
+    scale = r.V4[...].astype(F32).reshape(1, HD)
     factor = soft_unit / math.sqrt(HD) * (
         jnp.maximum(scale, 0.0) + jnp.log(1.0 + jnp.exp(-jnp.abs(scale)))
     )
@@ -808,7 +815,7 @@
             y_first,
         )
 
-    s_dn = w2_item(1, D, D, mine, True)
+    s_dn = w2_item(1, D, D, None, False)
     WZ = D // 2
     s_out = w2_item(2, 0, WZ, None, False)
     s_out2 = w2_item(5, WZ, D - WZ, mine, True) if WZ < D else ((lambda d: None), (lambda d: None))
@@ -823,8 +830,8 @@
     to_x(1, 1)
     dy_all = r.DY[...].reshape(L, D)
     r.G2[:, :, pl.ds(D, D)] = tn(r.ACT[...], dy_all).astype(BF16).reshape(nz, CB, D)
-    for d in (*far, 0):
-        s_dn[0](d)
+    if nz > 3:
+        s_dn[1](3)
 
     def back_middle(p):
         dh = pair_sum(1, p)
@@ -883,13 +890,12 @@
         back_attend(0, j)
     if nz > 2:
         s_up[1](2)
+        s_dn[1](2)
     wait_da = back_middle(1)
     r.XS[4] = chip_sum(2, 1 - x).astype(BF16)
     send(lambda: xcopy(2, 0))
     r.PF2[...] = chip_sum(2, x)
     s_up[1](1)
-    if nz > 3:
-        s_dn[1](3)
     wait_da()
     back_out(1)
     da_all = r.DA[...].reshape(L, D)
@@ -900,6 +906,7 @@
         s_out2[0](d)
     for j in range(NH):
         back_attend(1, j)
+    s_dn[1](1)
 
     def qkv_block(bb):
         t = nn(r.HN1T[bb], r.DQ[...]).reshape(2, CB, D - LO)
@@ -914,7 +921,6 @@
         s_own[0](d)
     qkv_block(2 * z + (1 - y))
     s_far[0](0)
-    s_own[0](0)
     for k in range(nz):
         qkv_block(2 * k + y)
 
@@ -922,22 +928,25 @@
         w = W1[:, :, :, pl.ds(LO, D - LO)].reshape(D, D - LO)
         to_sibling(3, p, nt(r.DQ[rows_of(p)], w))
     s_up[1](0)
-    if nz > 2:
-        s_dn[1](2)
     arrive(lambda: xcopy(2, 0))
     own_out = r.PF2[...] + r.XR[4].astype(F32)
     mixed_o[...] = (r.MID[x] + own_out + bias_down).astype(BF16)
     r.XS[5] = chip_sum(3, 1 - x).astype(BF16)
     send(lambda: xcopy(3, 0))
     r.PF2[...] = chip_sum(3, x)
-    s_dn[1](1)
+    s_dn[1](0)
+    cut_d = pl.ds(D, D)
+    m_gyd = lambda: copy(
+        r.G2.at[z, :, cut_d], r.YR2.at[z, :, cut_d], r.s_one.at[16], r.r_one.at[16], yp
+    )
+    send(m_gyd, not_mine)
+    s_own[0](0)
     if nz > 2:
         s_out[1](2)
     if nz > 3:
         s_out2[1](3)
         s_far[1](3)
         s_own[1](3)
-    s_dn[1](0)
     if nz > 2:
         s_far[1](2)
     s_out[1](1)
@@ -1019,9 +1028,11 @@
         owns[h][1](0)
         takes.append(hand_over(1, h, x, r.G1[b, x, :, ends[h]]))
     arrive(m_gy, mine)
+    arrive(m_gyd, mine)
 
     def out_from_y():
-        r.G2[z, :, cut_o] = (r.G2[z, :, cut_o].astype(F32) + r.YR2[z, :, cut_o].astype(F32)).astype(BF16)
+        for cut in (cut_o, cut_d):
+            r.G2[z, :, cut] = (r.G2[z, :, cut].astype(F32) + r.YR2[z, :, cut].astype(F32)).astype(BF16)
 
     when(mine, out_from_y)
     done2 = r.G2[z].astype(F32)
@@ -1062,6 +1073,11 @@
         WO=V((rows, D), BF16),
         WD=V((rows, D), BF16),
         SM=V((8, 128), F32),
+        V0=V((rows,), BF16),
+        V1=V((rows,), BF16),
+        V2=V((rows,), BF16),
+        V3=V((rows,), BF16),
+        V4=V((HD,), BF16),
         W1P=V((2, 2, 48, D), BF16),
         W2P=V((48, 2 * D), BF16),
         SIB1=V((2, 48, D), BF16),
@@ -1122,11 +1138,11 @@
     )
     dma = pltpu.SemaphoreType.DMA
     scratch.update(
-        s_in=dma((6,)),
+        s_in=dma((11,)),
         s_x1=dma((3,)), r_x1=dma((3,)),
         s_gf=dma((2, 2)), r_gf=dma((2, 2)),
         s_fx=dma((2,)), r_fx=dma((2,)),
-        s_one=dma((16,)), r_one=dma((16,)),
+        s_one=dma((17,)), r_one=dma((17,)),
         s_up=dma((9, nz)), r_up=dma((9, nz)),
         s_dn=dma((9, nz)), r_dn=dma((9, nz)),
         s_y=dma((9, nz)), r_y=dma((9, nz)),
@@ -1149,7 +1165,7 @@
             jax.ShapeDtypeStruct((rows, 2 * D), F32),
             jax.ShapeDtypeStruct((8, D), F32),
         ),
-        in_specs=[hbm] * 6 + [vmem] * 5,
+        in_specs=[hbm] * 11,
         out_specs=(vmem,) * 5,
         scratch_shapes=list(scratch.values()),
         compiler_params=pltpu.CompilerParams(

time: 140 us -> 138 us (0.986)
  no operation moved by 1% of the time
where the time goes in v5:
time: 138 us
  Pallas kernels  137 us (99%)
    pallas_call x1, Pallas kernels, fused_layer(): pl.pallas_call(functools.partial(layer_kernel, nz, tuple(scratch)), out_s...  133 us
    pallas_call x1, Pallas kernels, fused_layer(): pl.pallas_call(functools.partial(outputs_kernel, ns), out_shape=(jax.Shap...  3.51 us

profile of v5, /device:TPU:0, one launch (start us, length us, event | category | flops | bytes accessed | tf_op | source)
XLA Modules:
  0.0 137.8 jit_solution(3153868624165500376)
XLA Ops:
  0.6 133.4 %decoder_layer.1 = (bf16[128,1280]{1,0:T(8,128)(2,1)}, f32[128,1280]{1,0:T(8,128)}, f32[2,2,40,1280]{3,2,1,0:T(8,128)}, f32[40,2560]{1,0:T(8,128)}, f32[8,1280]{1,0:T(8,128)}) custom-call(bf16[128,1280]{1,0:T(8,128)(2,1)} %bitcast.4, bf16[128,1280]{1,0:T(8,128)(2,1)} %bitcast.5, bf16[40,3840]{1,0:T(8,128)(2,1)} %wqkv.1, bf16[40,1280]{1,0:T(8,128)(2,1)} %wout.1, ...), custom_call_target="tpu_custom_call" | custom-call | tf_op jit(solution)/shard_map/decoder_layer/pallas_call | solution.py:1159
  134.1 3.5 %place_outputs.1 = (bf16[128,1280]{1,0:T(8,128)(2,1)}, f32[128,1280]{1,0:T(8,128)}, f32[40,3840]{1,0:T(8,128)}, f32[40,1280]{1,0:T(8,128)}, f32[40,1280]{1,0:T(8...) custom-call(bf16[128,1280]{1,0:T(8,128)(2,1)} %get-tuple-element.27., ...), custom_call_target="tpu_custom_call" | custom-call | tf_op jit(solution)/shard_map/place_outputs/pallas_call | solution.py:1176

commit v6 on v5

--- a/solution.py
+++ b/solution.py
@@ -816,7 +816,7 @@
         )
 
     s_dn = w2_item(1, D, D, None, False)
-    WZ = D // 2
+    WZ = 2 * D // 5
     s_out = w2_item(2, 0, WZ, None, False)
     s_out2 = w2_item(5, WZ, D - WZ, mine, True) if WZ < D else ((lambda d: None), (lambda d: None))
     fars = [qkv_item(3, 1 - x, cuts[0]), qkv_item(6, 1 - x, cuts[1])]

time: 138 us -> 139 us (level)
  no operation moved by 1% of the time
where the time goes in v6:
time: 139 us; the launch traced here: 138 us
  Pallas kernels  138 us (99%)
    pallas_call x1, Pallas kernels, fused_layer(): pl.pallas_call(functools.partial(layer_kernel, nz, tuple(scratch)), out_s...  134 us
    pallas_call x1, Pallas kernels, fused_layer(): pl.pallas_call(functools.partial(outputs_kernel, ns), out_shape=(jax.Shap...  3.51 us

profile of v6, /device:TPU:0, one launch (start us, length us, event | category | flops | bytes accessed | tf_op | source)
XLA Modules:
  0.0 138.5 jit_solution(1770924331072841433)
XLA Ops:
  0.6 134.1 %decoder_layer.1 = (bf16[128,1280]{1,0:T(8,128)(2,1)}, f32[128,1280]{1,0:T(8,128)}, f32[2,2,40,1280]{3,2,1,0:T(8,128)}, f32[40,2560]{1,0:T(8,128)}, f32[8,1280]{1,0:T(8,128)}) custom-call(bf16[128,1280]{1,0:T(8,128)(2,1)} %bitcast.4, bf16[128,1280]{1,0:T(8,128)(2,1)} %bitcast.5, bf16[40,3840]{1,0:T(8,128)(2,1)} %wqkv.1, bf16[40,1280]{1,0:T(8,128)(2,1)} %wout.1, ...), custom_call_target="tpu_custom_call" | custom-call | tf_op jit(solution)/shard_map/decoder_layer/pallas_call | solution.py:1159
  134.8 3.5 %place_outputs.1 = (bf16[128,1280]{1,0:T(8,128)(2,1)}, f32[128,1280]{1,0:T(8,128)}, f32[40,3840]{1,0:T(8,128)}, f32[40,1280]{1,0:T(8,128)}, f32[40,1280]{1,0:T(8...) custom-call(bf16[128,1280]{1,0:T(8,128)(2,1)} %get-tuple-element.27., ...), custom_call_target="tpu_custom_call" | custom-call | tf_op jit(solution)/shard_map/place_outputs/pallas_call | solution.py:1176
